TPU v7x, 256 devices: a whole 4x4x8 slice. The times are simulated.
256 devices in a mesh: dp: 16 (over y, z_lo, core), tensor: 16 (over x, z_hi).
Axes of the slice: x: 4, y: 4, z: 8 (z_hi: 4, z_lo: 2; z = z_hi * 2 + z_lo), core: 2. Of those that a mesh axis runs over, the one named last changes fastest.
Arguments:
- inputs: bfloat16 [32768, 1664], P(('dp', 'tensor')), may hold values from -24 to 24
- gain: bfloat16 [1664], replicated, may hold values from 0.099609375 to 1.8984375
- w_up: bfloat16 [1664, 6400], P(None, 'tensor'), may hold values from -0.15625 to 0.15625
- w_down: bfloat16 [6400, 1664], P('tensor'), may hold values from -0.078125 to 0.078125
- upstream: bfloat16 [32768, 1664], P(('dp', 'tensor')), may hold values from -24 to 24
Outputs:
- input_grad: bfloat16 [32768, 1664], P(('dp', 'tensor'))
- up_grad: float32 [1664, 6400], P('dp', 'tensor')
- down_grad: float32 [6400, 1664], P('tensor', 'dp')
All inputs are finite; a program needn't handle non-finite values.
Results may differ from a plain program's by a relative error of at most 0.022.
Values may be sent and summed in bfloat16 or wider, within the bound.
A program may use at most 64 MiB of HBM per device.

v0:
```python
import jax
import jax.numpy as jnp
from jax import lax
from jax.sharding import PartitionSpec as P

norm_eps = 1e-06


def gelu_parts(pre):
    cdf = 0.5 * (1.0 + lax.erf(pre * 0.7071067811865476))
    pdf = jnp.exp(-0.5 * pre * pre) * 0.3989422804014327
    return (pre * cdf, cdf + pre * pdf)


def contract_rows(left, right):
    return lax.dot_general(
        left, right, (((0,), (0,)), ((), ())), preferred_element_type=jnp.float32
    )


def contract_cols(left, right):
    return lax.dot_general(
        left, right, (((1,), (1,)), ((), ())), preferred_element_type=jnp.float32
    )


def body(inputs, gain, w_up, w_down, upstream):
    tok_rows = inputs.shape[0]
    tensor_size = lax.axis_size("tensor")
    data_size = lax.axis_size("dp")
    grad_scale = float(tok_rows * tensor_size * data_size) ** (-0.5)
    gain_wide = gain.astype(jnp.float32)
    inputs_wide = inputs.astype(jnp.float32)
    inv_rms = lax.rsqrt(jnp.mean(inputs_wide * inputs_wide, axis=-1, keepdims=True) + norm_eps)
    unit_rows = inputs_wide * inv_rms
    normed = (unit_rows * gain_wide).astype(jnp.bfloat16)
    normed_all = lax.all_gather(normed, "tensor", axis=0, tiled=True)
    pre = jnp.dot(normed_all, w_up, preferred_element_type=jnp.float32)
    hidden_full, slope = gelu_parts(pre)
    hidden = hidden_full.astype(jnp.bfloat16)
    upstream_all = lax.all_gather(upstream, "tensor", axis=0, tiled=True)
    dhidden = contract_cols(upstream_all, w_down)
    dpre = (dhidden * slope).astype(jnp.bfloat16)
    down_term = contract_rows(hidden, upstream_all) * grad_scale
    up_term = contract_rows(normed_all, dpre)
    up_term = up_term * grad_scale
    dnormed = lax.psum_scatter(
        contract_cols(dpre, w_up).astype(jnp.bfloat16), "tensor", scatter_dimension=0, tiled=True
    ).astype(jnp.float32)
    up_grad, down_grad = (
        lax.psum_scatter(
            up_term.astype(jnp.bfloat16), "dp", scatter_dimension=0, tiled=True
        ).astype(jnp.float32),
        lax.psum_scatter(
            down_term.astype(jnp.bfloat16), "dp", scatter_dimension=1, tiled=True
        ).astype(jnp.float32),
    )
    dunit = dnormed * gain_wide
    project = jnp.mean(dunit * unit_rows, axis=-1, keepdims=True)
    grad_rows = upstream.astype(jnp.float32) + inv_rms * (dunit - unit_rows * project)
    return (grad_rows.astype(jnp.bfloat16), up_grad, down_grad)


def solution(mesh):
    in_specs = (
        P(("dp", "tensor"), None),
        P(),
        P(None, "tensor"),
        P("tensor", None),
        P(("dp", "tensor"), None),
    )
    out_specs = (P(("dp", "tensor"), None), P("dp", "tensor"), P("tensor", "dp"))
    return jax.shard_map(body, mesh=mesh, in_specs=in_specs, out_specs=out_specs, check_vma=False)
```

profile of v0, /device:TPU:1, one launch (start us, length us, event | category | flops | bytes accessed | tf_op | source)
XLA Modules:
  0.0 488.1 jit_solution(9449059971277481166)
XLA Ops:
  7.2 0.0 all-gather.5.cloned.1.call-start
  7.2 1.3 fusion.17
  8.5 0.7 convert_element_type.41
  9.2 1.9 fusion.11
  11.1 0.0 all-gather.5.cloned.1.call-update
  11.2 0.0 all-gather.3.cloned.1.call-start
  11.2 0.7 all-gather.3.cloned.1.call-update
  11.9 0.0 reduce-scatter.10.cloned.1.call-start
  12.0 96.8 %all-gather.5.cloned.1.call-done = bf16[2048,1664]{1,0:T(8,128)(2,1)} async-done(((bf16[128,1664]{1,0:T(8,128)(2,1)}), bf16[2048,1664]{1,0:T(8,128)(2,1)}) %all-gather.5.cloned.1.call-update) | async-done | bytes 6815760 | tf_op jit(solution)/shard_map/all_gather | solution.py:37
  108.7 7.7 %fusion.18 = f32[2048,400]{0,1:T(8,128)} fusion(bf16[2048,1664]{1,0:T(8,128)(2,1)} %all-gather.5.cloned.1.call-done, bf16[1664,400]{0,1:T(8,128)(2,1)S(1)} %copy-done), kind=kOutput, calls=%fused_computation.29 | convolution fusion | flops 2726297600 | bytes 11423744 | tf_op jit(solution)/shard_map/dot_general | solution.py:38
  116.5 94.8 %all-gather.3.cloned.1.call-done = bf16[2048,1664]{1,0:T(8,128)(2,1)} async-done(((bf16[128,1664]{1,0:T(8,128)(2,1)}), bf16[2048,1664]{1,0:T(8,128)(2,1)}) %all-gather.3.cloned.1.call-update) | async-done | bytes 6815760 | tf_op jit(solution)/shard_map/all_gather | solution.py:41
  211.2 8.6 %fusion.5 = bf16[2048,400]{0,1:T(8,128)(2,1)S(1)} fusion(f32[2048,400]{0,1:T(8,128)} %fusion.18, bf16[2048,1664]{1,0:T(8,128)(2,1)} %all-gather.3.cloned.1.call-done, bf16[400,1664]{1,0:T(8,128)(2,1)S(1)} %copy-done.4), kind=kOutput, calls=%fused_computation.7 | convolution fusion | flops 2734489600 | bytes 13062144 | tf_op jit(solution)/shard_map/dot_general | solution.py:22
  219.8 1.2 copy-done.5
  221.0 3.1 fusion.7
  224.1 2.3 copy.8
  226.4 0.0 reduce-scatter.10.cloned.1.call-update
  226.4 0.0 reduce-scatter.12.cloned.1.call-start
  226.5 7.2 %fusion.6 = bf16[400,1664]{1,0:T(8,128)(2,1)S(1)} fusion(bf16[2048,1664]{1,0:T(8,128)(2,1)} %all-gather.3.cloned.1.call-done, f32[2048,400]{0,1:T(8,128)} %fusion.18), kind=kOutput, calls=%fused_computation.12 | convolution fusion | flops 2731724800 | bytes 11423744 | tf_op jit(solution)/shard_map/dot_general | solution.py:16
  233.7 2.3 copy.10
  236.1 0.0 reduce-scatter.12.cloned.1.call-update
  236.1 0.2 reduce-scatter.8.cloned.1.call-start
  236.3 8.2 %convolution_convert_fusion = bf16[2048,1664]{1,0:T(8,128)(2,1)} fusion(bf16[2048,400]{0,1:T(8,128)(2,1)} %copy-done.5, bf16[1664,400]{0,1:T(8,128)(2,1)S(1)} %copy-done), kind=kOutput, calls=%fused_computation | convolution fusion | flops 2729705472 | bytes 9785344 | tf_op jit(solution)/shard_map/dot_general | solution.py:22
  244.6 0.0 reduce-scatter.8.cloned.1.call-update
  244.6 50.5 %reduce-scatter.10.cloned.1.call-done = bf16[104,400]{1,0:T(8,128)(2,1)} async-done(((bf16[1664,400]{1,0:T(8,128)(2,1)}), bf16[104,400]{1,0:T(8,128)(2,1)}) %reduce-scatter.10.cloned.1.call-update) | async-done | bytes 83216
  295.1 1.0 copy.9
  296.1 0.7 convert_element_type.48
  296.8 64.7 %reduce-scatter.12.cloned.1.call-done = bf16[104,400]{1,0:T(8,128)(2,1)} async-done(((bf16[1664,400]{1,0:T(8,128)(2,1)}), bf16[104,400]{1,0:T(8,128)(2,1)}) %reduce-scatter.12.cloned.1.call-update) | async-done | bytes 83216
  361.5 1.0 copy.11
  362.5 0.7 convert_element_type.51
  363.2 114.9 %reduce-scatter.8.cloned.1.call-done = bf16[128,1664]{1,0:T(8,128)(2,1)} async-done(((bf16[2048,1664]{1,0:T(8,128)(2,1)}), bf16[128,1664]{1,0:T(8,128)(2,1)}) %reduce-scatter.8.cloned.1.call-update) | async-done | bytes 426000 | tf_op jit(solution)/shard_map/reduce_scatter | solution.py:47
  478.2 1.3 fusion.12
  479.5 2.1 fusion.16
  (13 shorter events, 0.0 us)
Async XLA Ops:
  7.2 101.6 %copy-start = (bf16[1664,400]{0,1:T(8,128)(2,1)S(1)}, bf16[1664,400]{0,1:T(8,128)(2,1)}, u32[]{:S(2)}) copy-start(bf16[1664,400]{0,1:T(8,128)(2,1)} %param.7) | copy-start | bytes 3993604
  7.2 101.5 %all-gather.5.cloned.1.call-start = ((), (), s32[]{:S(2)}) async-start(), calls=%async_computation.4 | async-start | bytes 7241728 | tf_op jit(solution)/shard_map/all_gather | solution.py:37
  11.2 200.1 %all-gather.3.cloned.1.call-start = ((), (), s32[]{:S(2)}) async-start(), calls=%async_computation.3 | async-start | bytes 7241728 | tf_op jit(solution)/shard_map/all_gather | solution.py:41
  11.9 199.3 %copy-start.4 = (bf16[400,1664]{1,0:T(8,128)(2,1)S(1)}, bf16[400,1664]{1,0:T(8,128)(2,1)}, u32[]{:S(2)}) copy-start(bf16[400,1664]{1,0:T(8,128)(2,1)} %param.8) | copy-start | bytes 3993604
  11.9 283.2 %reduce-scatter.10.cloned.1.call-start = ((), (), s32[]{:S(2)}) async-start(), calls=%async_computation.6 | async-start | bytes 1810432
  211.2 9.8 %copy-start.3 = (bf16[2048,1664]{1,0:T(8,128)(2,1)S(1)}, bf16[2048,1664]{1,0:T(8,128)(2,1)}, u32[]{:S(2)}) copy-start(bf16[2048,1664]{1,0:T(8,128)(2,1)} %all-gather.5.cloned.1.call-done) | copy-start | bytes 20447236
  219.8 1.2 copy-start.5
  226.4 135.1 %reduce-scatter.12.cloned.1.call-start = ((), (), s32[]{:S(2)}) async-start(), calls=%async_computation.7 | async-start | bytes 1810432
  236.1 242.1 %reduce-scatter.8.cloned.1.call-start = ((), (), s32[]{:S(2)}) async-start(), calls=%async_computation.5 | async-start | bytes 7241728 | tf_op jit(solution)/shard_map/reduce_scatter | solution.py:47
  244.6 233.6 %copy-start.1 = (bf16[128,1664]{1,0:T(8,128)(2,1)S(1)}, bf16[128,1664]{1,0:T(8,128)(2,1)}, u32[]{:S(2)}) copy-start(bf16[128,1664]{1,0:T(8,128)(2,1)} %param.5) | copy-start | bytes 1277956
  244.6 234.9 %copy-start.2 = (bf16[128,1664]{1,0:T(8,128)(2,1)S(1)}, bf16[128,1664]{1,0:T(8,128)(2,1)}, u32[]{:S(2)}) copy-start(bf16[128,1664]{1,0:T(8,128)(2,1)} %param.9) | copy-start | bytes 1277956
Sparse Core Ops, SparseCore 0:
  11.3 97.4 all-gather.4
  111.2 99.9 all-gather.2
  226.6 68.4 reduce-scatter.9
  297.7 63.8 reduce-scatter.11
  365.1 113.0 reduce-scatter.7
where the time goes:
time: 489 us; the launch traced here: 488 us
  waiting for transfers between devices  422 us (86%)
  matrix products  34.9 us (7%)
  between operations  13.8 us (3%)
  other arithmetic  8.72 us (2%)
  local copies, waits for them, and re-layouts  7.86 us (2%)
    unnamed x7, waiting for transfers between devices  116 us
    reduce_scatter x1, waiting for transfers between devices, body(): lax.psum_scatter(contract_cols(dpre, w_up).astype(jnp.bfloat16), 'tensor'...  115 us
    all_gather x1, waiting for transfers between devices, body(): normed_all = lax.all_gather(normed, 'tensor', axis=0, tiled=True)  96.8 us
    all_gather x1, waiting for transfers between devices, body(): upstream_all = lax.all_gather(upstream, 'tensor', axis=0, tiled=True)  94.8 us
    dot_general x2, matrix products, contract_cols(): lax.dot_general(left, right, (((1,), (1,)), ((), ())), preferred_element_...  16.8 us
    dot_general x2, matrix products, contract_rows(): lax.dot_general(left, right, (((0,), (0,)), ((), ())), preferred_element_...  10.3 us
  transfers between devices with their start and end apart: 5, of which 5 were waited for; matrix products, arithmetic and copies ran while one was open for 6% of the time, Pallas kernels for 0%

commit v1 on v0

v1 whole, which is shorter than its diff:
```python
import jax
import jax.numpy as jnp
from jax import lax
from jax.experimental import pallas as pl
from jax.experimental.pallas import tpu as pltpu
from jax.sharding import PartitionSpec as P

MESH = pl.DeviceIdType.MESH
F32, BF16 = jnp.float32, jnp.bfloat16

norm_eps = 1e-06
D = 1664
TOK = 128
GROUP = 2 * TOK
T = 4 * GROUP
HALF = 208
HID = 4 * HALF
WIN = 512
CHUNKS = ((0, 64), (64, 48), (112, 48), (160, 48))
N_SEM = 80
GRAD_SCALE = float(32768) ** (-0.5)

MIRROR = {0: 0, 1: 3, 2: 2, 3: 1}


def gelu_parts(pre):
    cdf = 0.5 * (1.0 + lax.erf(pre * 0.7071067811865476))
    pdf = jnp.exp(-0.5 * pre * pre) * 0.3989422804014327
    return (pre * cdf, cdf + pre * pdf)


def place(x, y, z, c):
    x, y, z = (x + 8) % 4, (y + 8) % 4, (z + 16) % 8
    return (y * 4 + (z % 2) * 2 + c, x * 4 + z // 2)


def kernel(
    x_ref, up_ref, gain_ref, w_ref, grad_ref, out_ref,
    tok_n, tok_u, w, hid, dpre, g, yo_in, ya_st, nb_in, ysum, z1_in, z2_st, z2_in, total, fin_st, fin_in,
    dn, dn_sib, dn_st, dn_in, ss, rs, local_sem,
):
    dp, tensor = lax.axis_index("dp"), lax.axis_index("tensor")
    y, zl, c = dp // 4, (dp // 2) % 2, dp % 2
    x, z = tensor // 4, (tensor % 4) * 2 + zl
    step_out = 2 * zl - 1
    sib = place(x, y, z, 1 - c)
    xr, xl = place(x + 1, y, z, c), place(x - 1, y, z, c)
    x_far = place(x + 2, y, z, c)
    yr, yl = place(x, y + 1, z, c), place(x, y - 1, z, c)
    z_out, z_in = place(x, y, z + step_out, c), place(x, y, z - step_out, c)
    z_cross = place(x, y, z - step_out, 1 - c)
    z_far = {1: place(x, y, z + 2 * step_out, c), 2: place(x, y, z + 4, c), 3: place(x, y, z - 2 * step_out, c)}
    kind_out, kind_in = zl, 1 - zl
    mine = zl

    own_w = pltpu.make_async_copy(w_ref, w.at[:, pl.ds(0, HALF)], local_sem)
    own_w.start()
    barrier = pltpu.get_barrier_semaphore()
    peers = [sib, xr, xl, x_far, yr, yl, z_out, z_in, z_cross, z_far[1], z_far[2], z_far[3]]
    for peer in peers:
        pl.semaphore_signal(barrier, inc=1, device_id=peer, device_id_type=MESH)

    copies = {}

    def send(key, src, dst, device):
        i = len(copies)
        copies[key] = pltpu.make_async_remote_copy(
            src_ref=src, dst_ref=dst, send_sem=ss.at[i], recv_sem=rs.at[i], device_id=device, device_id_type=MESH
        )
        copies[key].start()

    def recv(*keys):
        for key in keys:
            copies[key].wait_recv()

    def tok_rows(group, core, first=0, rows=TOK):
        return pl.ds(pl.multiple_of(group * GROUP + core * TOK + first, 16), rows)

    def norm(i, _):
        r = pl.ds(pl.multiple_of(i * 16, 16), 16)
        wide = x_ref[r].astype(F32)
        inv = lax.rsqrt(jnp.mean(wide * wide, axis=-1, keepdims=True) + norm_eps)
        to = pl.ds(pl.multiple_of(c * TOK + i * 16, 16), 16)
        tok_n[to] = (wide * inv * gain_ref[...]).astype(BF16)
        tok_u[to] = up_ref[r]
        return 0

    lax.fori_loop(0, TOK // 16, norm, 0)
    pl.semaphore_wait(barrier, len(peers))

    toks = {"u": tok_u, "n": tok_n}
    own = tok_rows(0, c)
    for a in ("u", "n"):
        send((a, "r"), toks[a].at[own], toks[a].at[tok_rows(3, c)], xr)
        send((a, "l"), toks[a].at[own], toks[a].at[tok_rows(1, c)], xl)
        send((a, "s0"), toks[a].at[own], toks[a].at[own], sib)
    own_w.wait()

    def chunk(slot, i):
        first, rows = CHUNKS[i]
        return pl.ds(slot * HALF + first, rows)

    for i in range(4):
        send(("w0", i), w.at[:, chunk(0, i)], w.at[:, chunk(1, i)], z_out)

    def pass_neighbours(a):
        recv((a, "r"))
        send((a, "fr"), toks[a].at[tok_rows(3, c, 0, 64)], toks[a].at[tok_rows(2, c, 0, 64)], xr)
        send((a, "s3"), toks[a].at[tok_rows(3, c)], toks[a].at[tok_rows(3, c)], sib)
        recv((a, "l"))
        send((a, "fl"), toks[a].at[tok_rows(1, c, 64, 64)], toks[a].at[tok_rows(2, c, 64, 64)], xl)
        send((a, "s1"), toks[a].at[tok_rows(1, c)], toks[a].at[tok_rows(1, c)], sib)

    def pass_opposite(a):
        recv((a, "fr"), (a, "fl"))
        send((a, "s2"), toks[a].at[tok_rows(2, c)], toks[a].at[tok_rows(2, c)], sib)

    def pass_w1(i):
        recv(("w0", i))
        send(("w1", i), w.at[:, chunk(1, i)], w.at[:, chunk(3, i)], z_in)

    def pass_w3(i):
        recv(("w1", i))
        send(("w3", i), w.at[kind_in, chunk(3, i)], w.at[kind_in, chunk(2, i)], z_out)

    def pass_w2(i):
        recv(("w3", i))
        send(("w2", i), w.at[kind_out, chunk(2, i)], w.at[kind_out, chunk(2, i)], z_in)

    def forward(slot, group):
        r = pl.ds(slot * HALF, HALF)
        t = pl.ds(pl.multiple_of(group * GROUP, GROUP), GROUP)
        nt = (((1,), (1,)), ((), ()))
        pre = lax.dot_general(w[0, r], tok_n[t], nt, preferred_element_type=F32)
        dhidden = lax.dot_general(w[1, r], tok_u[t], nt, preferred_element_type=F32)
        hidden, slope = gelu_parts(pre)
        hid[r, t] = hidden.astype(BF16)
        dpre[r, t] = (dhidden * slope).astype(BF16)

    def forward_all(slot):
        def one(group, _):
            forward(slot, group)
            return 0

        lax.fori_loop(0, 4, one, 0)

    def grads(slot):
        r = pl.ds(slot * HALF, HALF)

        def columns(cols):
            up = jnp.dot(dpre[r], tok_n[:, cols], preferred_element_type=F32)
            g[0, r, cols] = (up * GRAD_SCALE).astype(BF16)
            down = jnp.dot(hid[r], tok_u[:, cols], preferred_element_type=F32)
            g[1, r, cols] = (down * GRAD_SCALE).astype(BF16)

        def tile(n, _):
            columns(pl.ds(pl.multiple_of(n * 256, 256), 256))
            return 0

        lax.fori_loop(0, 6, tile, 0)
        columns(pl.ds(1536, 128))

    def window(owner, first=0, cols=WIN):
        return pl.ds(pl.multiple_of(((owner + 8) % 4) * 384 + first, 128), cols)

    def y1(slot):
        r = pl.ds(slot * HALF, HALF)
        send(("yo", slot, 0), g.at[:, r, window(y + 2, 0, 256)], yo_in.at[slot, 0], yr)
        send(("yo", slot, 1), g.at[:, r, window(y + 2, 256, 256)], yo_in.at[slot, 1], yl)
        send(("yd", slot, 0), g.at[:, r, window(y + 1, 256, 256)], nb_in.at[slot, 0, :, :, pl.ds(256, 256)], yr)
        send(("yd", slot, 1), g.at[:, r, window(y - 1, 0, 256)], nb_in.at[slot, 1, :, :, pl.ds(0, 256)], yl)

    def rows16(i):
        return pl.ds(pl.multiple_of(i * 16, 16), 16)

    def y2(slot):
        for way, owner, first, peer in ((0, y + 1, 0, yr), (1, y - 1, 256, yl)):
            recv(("yo", slot, way))
            cols = window(owner, first, 256)

            def add(i, _):
                part = pl.ds(pl.multiple_of(slot * HALF + i * 16, 16), 16)
                here = rows16(i)
                ya_st[slot, way, :, here] = (
                    g[:, part, cols].astype(F32) + yo_in[slot, way, :, here].astype(F32)
                ).astype(BF16)
                return 0

            lax.fori_loop(0, HALF // 16, add, 0)
            send(("ya", slot, way), ya_st.at[slot, way], nb_in.at[slot, way, :, :, pl.ds(first, 256)], peer)

    def y3(slot):
        recv(("yd", slot, 0), ("yd", slot, 1), ("ya", slot, 0), ("ya", slot, 1))
        cols = window(y)

        def add(i, _):
            part = pl.ds(pl.multiple_of(slot * HALF + i * 16, 16), 16)
            here = rows16(i)
            ysum[slot, :, here] = (
                g[:, part, cols].astype(F32)
                + nb_in[slot, 0, :, here].astype(F32)
                + nb_in[slot, 1, :, here].astype(F32)
            ).astype(BF16)
            return 0

        lax.fori_loop(0, HALF // 16, add, 0)
        there = MIRROR[slot]
        send(("z1", there), ysum.at[slot, 1 - mine], z1_in.at[there], z_in)

    def z2(slot):
        recv(("z1", slot))

        def add(i, _):
            here = rows16(i)
            z2_st[slot - 1, here] = (
                ysum[slot, mine, here].astype(F32) + z1_in[slot, here].astype(F32)
            ).astype(BF16)
            return 0

        lax.fori_loop(0, HALF // 16, add, 0)
        send(("z2", slot), z2_st.at[slot - 1], z2_in.at[slot - 1], z_far[slot])

    def back(group):
        t = pl.ds(group * GROUP, GROUP)
        rows = dpre[:, t].T

        def columns(cols):
            part = jnp.dot(rows, w[0, :, cols], preferred_element_type=F32).astype(BF16)
            dn[group, 0, :, cols] = part[:TOK]
            dn[group, 1, :, cols] = part[TOK:]

        def tile(n, _):
            columns(pl.ds(pl.multiple_of(n * 256, 256), 256))
            return 0

        lax.fori_loop(0, 6, tile, 0)
        columns(pl.ds(1536, 128))
        send(("dn", group), dn.at[group, 1 - c], dn_sib.at[group], sib)

    def dn_pass(group, peer):
        recv(("dn", group))

        def add(i, _):
            here = rows16(i)
            dn_st[group - 1, here] = (dn[group, c, here].astype(F32) + dn_sib[group, here].astype(F32)).astype(BF16)
            return 0

        lax.fori_loop(0, TOK // 16, add, 0)
        send(("dx", group), dn_st.at[group - 1], dn_in.at[group - 1], peer)

    pass_neighbours("u")
    pass_w1(0)
    recv(("u", "s0"), ("n", "s0"))
    forward(0, 0)
    pass_neighbours("n")
    pass_w1(1)
    recv(("u", "s1"), ("n", "s1"))
    forward(0, 1)
    pass_w3(0)
    recv(("u", "s3"), ("n", "s3"))
    forward(0, 3)
    pass_w1(2)
    pass_opposite("u")
    pass_w2(0)
    pass_opposite("n")
    pass_w3(1)
    recv(("u", "s2"), ("n", "s2"))
    forward(0, 2)
    pass_w1(3)
    pass_w2(1)
    grads(0)
    y1(0)
    pass_w3(2)
    forward_all(1)
    pass_w2(2)
    pass_w3(3)
    grads(1)
    y1(1)
    y2(0)
    pass_w2(3)
    forward_all(3)
    grads(3)
    y1(3)
    y2(1)
    recv(("w2", 0), ("w2", 1), ("w2", 2), ("w2", 3))
    forward_all(2)
    grads(2)
    y1(2)
    y2(3)
    y3(0)
    back(2)
    back(1)
    y2(2)
    back(3)
    back(0)
    dn_pass(2, x_far)
    dn_pass(1, xr)
    dn_pass(3, xl)
    y3(1)
    y3(3)
    z2(1)
    z2(3)
    y3(2)
    z2(2)

    recv(("dn", 0), ("dx", 1), ("dx", 2), ("dx", 3))

    def finish(i, _):
        here = rows16(i)
        gain = gain_ref[...]
        wide = x_ref[here].astype(F32)
        inv = lax.rsqrt(jnp.mean(wide * wide, axis=-1, keepdims=True) + norm_eps)
        unit = wide * inv
        dnormed = dn[0, c, here].astype(F32) + dn_sib[0, here].astype(F32)
        for k in range(3):
            dnormed += dn_in[k, here].astype(F32)
        dunit = dnormed * gain
        project = jnp.mean(dunit * unit, axis=-1, keepdims=True)
        grad_ref[here] = (up_ref[here].astype(F32) + inv * (dunit - unit * project)).astype(BF16)
        return 0

    lax.fori_loop(0, TOK // 16, finish, 0)

    recv(("z1", 0), ("z2", 1), ("z2", 2), ("z2", 3))
    total[:, pl.ds(WIN, 128)] = jnp.zeros((16, 128), F32)

    def split(i, _):
        here = rows16(i)
        rows = ysum[0, mine, here].astype(F32) + z1_in[0, here].astype(F32)
        for k in range(3):
            rows += z2_in[k, here].astype(F32)
        total[:, pl.ds(0, WIN)] = rows
        for q in range(4):
            turned = pltpu.roll(total[...], (WIN + 128 - 104 * q) - 32 * y, 1)
            fin_st[q, here] = turned[:, :128].astype(BF16)
        return 0

    lax.fori_loop(0, HALF // 16, split, 0)
    me = 2 * zl + c
    for key, device, to in (("sib", sib, 2 * zl + 1 - c), ("in", z_in, 2 * (1 - zl) + c), ("cross", z_cross, 2 * (1 - zl) + 1 - c)):
        send(("f", key), fin_st.at[to], fin_in.at[me], device)

    def keep(i, _):
        fin_in[me, rows16(i)] = fin_st[me, rows16(i)]
        return 0

    lax.fori_loop(0, HALF // 16, keep, 0)
    recv(("f", "sib"), ("f", "in"), ("f", "cross"))

    def store(i, _):
        here = rows16(i)
        for q in range(4):
            out_ref[q, here] = fin_in[q, here].astype(F32)
        return 0

    lax.fori_loop(0, HALF // 16, store, 0)
    for copy in copies.values():
        copy.wait_send()


def body(inputs, gain, w_up, w_down, upstream):
    core = lax.axis_index("dp") % 2
    up_rows = jnp.pad(w_up, ((0, 0), (0, 16)))
    down_rows = jnp.pad(w_down, ((0, 16), (0, 0)))
    w_own = jnp.stack([
        lax.dynamic_slice_in_dim(up_rows, core * HALF, HALF, 1).T,
        lax.dynamic_slice_in_dim(down_rows, core * HALF, HALF, 0),
    ])
    vmem = pl.BlockSpec(memory_space=pltpu.VMEM)
    input_grad, pieces = pl.pallas_call(
        kernel,
        out_shape=(jax.ShapeDtypeStruct((TOK, D), BF16), jax.ShapeDtypeStruct((4, HALF, 128), F32)),
        in_specs=[vmem, vmem, vmem, pl.BlockSpec(memory_space=pl.ANY)],
        out_specs=(vmem, vmem),
        scratch_shapes=[
            pltpu.VMEM((T, D), BF16),
            pltpu.VMEM((T, D), BF16),
            pltpu.VMEM((2, HID, D), BF16),
            pltpu.VMEM((HID, T), BF16),
            pltpu.VMEM((HID, T), BF16),
            pltpu.VMEM((2, HID, D), BF16),
            pltpu.VMEM((4, 2, 2, HALF, 256), BF16),
            pltpu.VMEM((4, 2, 2, HALF, 256), BF16),
            pltpu.VMEM((4, 2, 2, HALF, WIN), BF16),
            pltpu.VMEM((4, 2, HALF, WIN), BF16),
            pltpu.VMEM((4, HALF, WIN), BF16),
            pltpu.VMEM((3, HALF, WIN), BF16),
            pltpu.VMEM((3, HALF, WIN), BF16),
            pltpu.VMEM((16, WIN + 128), F32),
            pltpu.VMEM((4, HALF, 128), BF16),
            pltpu.VMEM((4, HALF, 128), BF16),
            pltpu.VMEM((4, 2, TOK, D), BF16),
            pltpu.VMEM((4, TOK, D), BF16),
            pltpu.VMEM((3, TOK, D), BF16),
            pltpu.VMEM((3, TOK, D), BF16),
            pltpu.SemaphoreType.DMA((N_SEM,)),
            pltpu.SemaphoreType.DMA((N_SEM,)),
            pltpu.SemaphoreType.DMA,
        ],
        compiler_params=pltpu.CompilerParams(
            collective_id=1, has_side_effects=True, vmem_limit_bytes=60 * 2**20
        ),
        name="block_backward",
    )(inputs, upstream, gain.astype(F32).reshape(1, D), w_own)
    up_grad = pieces[:2].reshape(2 * HALF, 128)[:400, :104].T
    down_grad = pieces[2:].reshape(2 * HALF, 128)[:400, :104]
    return input_grad, up_grad, down_grad


def solution(mesh):
    in_specs = (
        P(("dp", "tensor"), None),
        P(),
        P(None, "tensor"),
        P("tensor", None),
        P(("dp", "tensor"), None),
    )
    out_specs = (P(("dp", "tensor"), None), P("dp", "tensor"), P("tensor", "dp"))
    return jax.shard_map(body, mesh=mesh, in_specs=in_specs, out_specs=out_specs, check_vma=False)
```

time: 489 us -> 155 us (0.32)
  waiting for transfers between devices: 422 us -> 0 us
  Pallas kernels: 0 us -> 147 us
  matrix products: 34.9 us -> 0 us
  between operations: 13.8 us -> 0.69 us
  other arithmetic: 8.72 us -> 1.25 us
    all_gather x2 -> x0, waiting for transfers between devices: 192 us -> none  [the longest x1 96.8 us: body(): normed_all = lax.all_gather(normed, 'tensor', axis=0, tiled=True)]
    pallas_call x0 -> x1, Pallas kernels: none -> 147 us  [body(): pl.pallas_call(kernel, out_shape=(jax.ShapeDtypeStruct((TOK, D), BF16), j...]
    unnamed x7 -> x0, waiting for transfers between devices: 116 us -> none
    reduce_scatter x1 -> x0, waiting for transfers between devices: 115 us -> none  [body(): lax.psum_scatter(contract_cols(dpre, w_up).astype(jnp.bfloat16), 'tensor'...]
    dot_general x5 -> x0, matrix products: 34.9 us -> none  [the longest x2 16.8 us: contract_cols(): lax.dot_general(left, right, (((1,), (1,)), ((), ())), preferred_element_...]
    unnamed x16 -> x7, local copies, waits for them, and re-layouts: 7.86 us -> 1.01 us
    convert_element_type x5 -> x0, other arithmetic: 6.14 us -> none  [the longest x1 2.11 us: body(): return (grad_rows.astype(jnp.bfloat16), up_grad, down_grad)]
  transfers between devices with their start and end apart: 5 -> 0, of which waited for: 5 -> 0; matrix products, arithmetic and copies ran while one was open for 6% -> 0% of each run, Pallas kernels for 0% -> 0%
where the time goes in v1:
time: 155 us
  Pallas kernels  147 us (95%)
  local copies, waits for them, and re-layouts  5.42 us (3%)
    pallas_call x1, Pallas kernels, body(): pl.pallas_call(kernel, out_shape=(jax.ShapeDtypeStruct((TOK, D), BF16), j...  147 us

profile of v1, /device:TPU:1, one launch (start us, length us, event | category | flops | bytes accessed | tf_op | source)
XLA Modules:
  0.0 154.6 jit_solution(17572989624420211345)
XLA Ops:
  0.6 0.0 copy-start
  0.7 1.2 fusion
  1.9 0.2 copy-done
  2.1 0.1 fusion.1
  2.2 0.0 copy-start.2
  2.2 1.3 pad_maximum_fusion.w_ref
  3.5 0.0 copy-done.2
  3.5 0.6 reshape.22.gain_ref
  4.1 147.3 %block_backward.1 = (bf16[128,1664]{1,0:T(8,128)(2,1)}, f32[4,208,128]{2,1,0:T(8,128)}) custom-call(bf16[128,1664]{1,0:T(8,128)(2,1)} %x_ref.1, bf16[128,1664]{1,0:T(8,128)(2,1)} %up_ref.1, f32[1,1664]{1,0:T(1,128)} %reshape.22.gain_ref, bf16[2,208,1664]{2,1,0:T(8,128)(2,1)} %pad_maximum_fusion.w_ref), custom_call_target="tpu_custom_call" | custom-call | tf_op jit(solution)/shard_map/block_backward/pallas_call | solution.py:370
  151.3 0.0 copy-start.1
  151.4 1.1 fusion.2
  152.5 0.7 slice.17
  153.2 0.7 slice_bitcast_fusion
  153.9 0.0 copy-done.1
  153.9 0.8 copy.9
Async XLA Ops:
  0.6 1.5 copy-start
  2.2 1.3 copy-start.2
  151.3 2.5 %copy-start.1 = (bf16[128,1664]{1,0:T(8,128)(2,1)S(1)}, bf16[128,1664]{1,0:T(8,128)(2,1)}, u32[]{:S(2)}) copy-start(bf16[128,1664]{1,0:T(8,128)(2,1)} %get-tuple-element.12) | copy-start | bytes 1277956

commit v2 on v1

--- a/solution.py
+++ b/solution.py
@@ -17,10 +17,8 @@
 HID = 4 * HALF
 WIN = 512
 CHUNKS = ((0, 64), (64, 48), (112, 48), (160, 48))
-N_SEM = 80
+N_SEM = 88
 GRAD_SCALE = float(32768) ** (-0.5)
-
-MIRROR = {0: 0, 1: 3, 2: 2, 3: 1}
 
 
 def gelu_parts(pre):
@@ -35,9 +33,9 @@
 
 
 def kernel(
-    x_ref, up_ref, gain_ref, w_ref, grad_ref, out_ref,
-    tok_n, tok_u, w, hid, dpre, g, yo_in, ya_st, nb_in, ysum, z1_in, z2_st, z2_in, total, fin_st, fin_in,
-    dn, dn_sib, dn_st, dn_in, ss, rs, local_sem,
+    x_ref, up_ref, gain_ref, wu_ref, wd_ref, grad_ref, up_out, down_out,
+    tok_n, tok_u, wt, w, hid, dpre, g, yo_in, ya_st, nb_in, ysum, za_in, zb_in, total, fin_st, fin_in, up_rows,
+    dn, dn_sib, dn_st, dn_in, ss, rs,
 ):
     dp, tensor = lax.axis_index("dp"), lax.axis_index("tensor")
     y, zl, c = dp // 4, (dp // 2) % 2, dp % 2
@@ -49,59 +47,91 @@
     yr, yl = place(x, y + 1, z, c), place(x, y - 1, z, c)
     z_out, z_in = place(x, y, z + step_out, c), place(x, y, z - step_out, c)
     z_cross = place(x, y, z - step_out, 1 - c)
-    z_far = {1: place(x, y, z + 2 * step_out, c), 2: place(x, y, z + 4, c), 3: place(x, y, z - 2 * step_out, c)}
-    kind_out, kind_in = zl, 1 - zl
+    z_same = {1: place(x, y, z + 2 * step_out, c), 2: place(x, y, z + 4, c), 3: place(x, y, z - 2 * step_out, c)}
+    z_other = {0: z_in, 1: z_out, 2: place(x, y, z + 3 * step_out, c), 3: place(x, y, z - 3 * step_out, c)}
+    kind = y % 2
+    from_out, from_in = 16 + 96 * zl, 112 - 96 * zl
     mine = zl
 
-    own_w = pltpu.make_async_copy(w_ref, w.at[:, pl.ds(0, HALF)], local_sem)
-    own_w.start()
     barrier = pltpu.get_barrier_semaphore()
-    peers = [sib, xr, xl, x_far, yr, yl, z_out, z_in, z_cross, z_far[1], z_far[2], z_far[3]]
+    peers = [sib, xr, xl, x_far, yr, yl, z_cross, *z_same.values(), *z_other.values()]
     for peer in peers:
         pl.semaphore_signal(barrier, inc=1, device_id=peer, device_id_type=MESH)
 
-    copies = {}
-
-    def send(key, src, dst, device):
+    copies, only = {}, {}
+
+    def make(key, src, dst, device):
         i = len(copies)
         copies[key] = pltpu.make_async_remote_copy(
             src_ref=src, dst_ref=dst, send_sem=ss.at[i], recv_sem=rs.at[i], device_id=device, device_id_type=MESH
         )
-        copies[key].start()
-
-    def recv(*keys):
+
+    def start(key, when=None):
+        if when is None:
+            copies[key].start()
+        else:
+            only[key] = when
+            pl.when(when)(copies[key].start)
+
+    def send(key, src, dst, device, when=None):
+        make(key, src, dst, device)
+        start(key, when)
+
+    def recv(*keys, when=None):
         for key in keys:
-            copies[key].wait_recv()
+            if when is None:
+                copies[key].wait_recv()
+            else:
+                pl.when(when)(copies[key].wait_recv)
 
     def tok_rows(group, core, first=0, rows=TOK):
         return pl.ds(pl.multiple_of(group * GROUP + core * TOK + first, 16), rows)
+
+    own = tok_rows(0, c)
+    tok_u[own] = up_ref[...]
+    toks = {"u": tok_u, "n": tok_n}
+
+    def send_own(a):
+        send((a, "r"), toks[a].at[own], toks[a].at[tok_rows(3, c)], xr)
+        send((a, "l"), toks[a].at[own], toks[a].at[tok_rows(1, c)], xl)
+        send((a, "s0"), toks[a].at[own], toks[a].at[own], sib)
+
+    pl.semaphore_wait(barrier, len(peers))
+    send_own("u")
+
+    for n in range(13):
+        cols = pl.ds(n * 128, 128)
+        wt[pl.ds(0, 400), cols] = wu_ref[cols, :].T
+    wt[pl.ds(400, 16)] = jnp.zeros((16, D), BF16)
+    w[0, pl.ds(0, HALF)] = wt[pl.ds(pl.multiple_of(c * HALF, 16), HALF)]
+
+    @pl.when(c == 0)
+    def _():
+        w[1, pl.ds(0, HALF)] = wd_ref[pl.ds(0, HALF)]
+
+    @pl.when(c == 1)
+    def _():
+        w[1, pl.ds(0, 192)] = wd_ref[pl.ds(HALF, 192)]
+        w[1, pl.ds(192, 16)] = jnp.zeros((16, D), BF16)
+
+    def rows_of(slot, first, rows):
+        return pl.ds(pl.multiple_of(slot * HALF + first, 16), rows)
+
+    def chunk(slot, i):
+        return rows_of(slot, *CHUNKS[i])
+
+    for i in range(4):
+        send(("w0", i), w.at[kind, chunk(0, i)], w.at[kind, chunk(1, i)], z_out)
 
     def norm(i, _):
         r = pl.ds(pl.multiple_of(i * 16, 16), 16)
         wide = x_ref[r].astype(F32)
         inv = lax.rsqrt(jnp.mean(wide * wide, axis=-1, keepdims=True) + norm_eps)
-        to = pl.ds(pl.multiple_of(c * TOK + i * 16, 16), 16)
-        tok_n[to] = (wide * inv * gain_ref[...]).astype(BF16)
-        tok_u[to] = up_ref[r]
+        tok_n[tok_rows(0, c, i * 16, 16)] = (wide * inv * gain_ref[...]).astype(BF16)
         return 0
 
     lax.fori_loop(0, TOK // 16, norm, 0)
-    pl.semaphore_wait(barrier, len(peers))
-
-    toks = {"u": tok_u, "n": tok_n}
-    own = tok_rows(0, c)
-    for a in ("u", "n"):
-        send((a, "r"), toks[a].at[own], toks[a].at[tok_rows(3, c)], xr)
-        send((a, "l"), toks[a].at[own], toks[a].at[tok_rows(1, c)], xl)
-        send((a, "s0"), toks[a].at[own], toks[a].at[own], sib)
-    own_w.wait()
-
-    def chunk(slot, i):
-        first, rows = CHUNKS[i]
-        return pl.ds(slot * HALF + first, rows)
-
-    for i in range(4):
-        send(("w0", i), w.at[:, chunk(0, i)], w.at[:, chunk(1, i)], z_out)
+    send_own("n")
 
     def pass_neighbours(a):
         recv((a, "r"))
@@ -115,17 +145,44 @@
         recv((a, "fr"), (a, "fl"))
         send((a, "s2"), toks[a].at[tok_rows(2, c)], toks[a].at[tok_rows(2, c)], sib)
 
+    def share(key, rows, peer):
+        send(("wy", key), w.at[kind, rows], w.at[kind, rows], peer)
+
     def pass_w1(i):
         recv(("w0", i))
-        send(("w1", i), w.at[:, chunk(1, i)], w.at[:, chunk(3, i)], z_in)
+        send(("w1", i), w.at[kind, chunk(1, i)], w.at[kind, chunk(3, i)], z_in)
+        share((1, i), chunk(1, i), (yr, yr, yl, yl)[i])
 
     def pass_w3(i):
         recv(("w1", i))
-        send(("w3", i), w.at[kind_in, chunk(3, i)], w.at[kind_in, chunk(2, i)], z_out)
-
-    def pass_w2(i):
-        recv(("w3", i))
-        send(("w2", i), w.at[kind_out, chunk(2, i)], w.at[kind_out, chunk(2, i)], z_in)
+        if i == 0:
+            extra = rows_of(3, 0, 16), rows_of(2, 0, 16)
+            send(("w3", "x"), w.at[kind, extra[0]], w.at[kind, extra[1]], z_out, zl == 1)
+            for n in range(2):
+                there = rows_of(2, from_in + 48 * n, 48)
+                make(("w3", n), w.at[kind, rows_of(3, from_in + 48 * n, 48)], w.at[kind, there], z_out)
+        pl.when(zl == 1 - i // 2)(copies["w3", i % 2].start)
+        share((3, i), chunk(3, i), (yl, yl, yr, yr)[i])
+
+    def pass_w2(n):
+        recv(("w3", n))
+        rows = rows_of(2, from_out + 48 * n, 48)
+        send(("w2", n), w.at[kind, rows], w.at[kind, rows], z_in)
+        share((2, "o", n), rows, yr)
+        if n == 1:
+            recv(("w3", "x"), when=zl == 0)
+            rows = rows_of(2, 0, 16)
+            send(("w2", "x"), w.at[kind, rows], w.at[kind, rows], z_in, zl == 0)
+
+    def pass_last():
+        for n in range(2):
+            recv(("w2", n))
+            share((2, "i", n), rows_of(2, from_in + 48 * n, 48), yl)
+        recv(("w2", "x"), when=zl == 1)
+        share((2, "x"), rows_of(2, 0, 16), yl)
+
+    def all_w(slot):
+        recv(*[key for key in copies if key[0] == "wy" and key[1][0] == slot])
 
     def forward(slot, group):
         r = pl.ds(slot * HALF, HALF)
@@ -204,21 +261,9 @@
             return 0
 
         lax.fori_loop(0, HALF // 16, add, 0)
-        there = MIRROR[slot]
-        send(("z1", there), ysum.at[slot, 1 - mine], z1_in.at[there], z_in)
-
-    def z2(slot):
-        recv(("z1", slot))
-
-        def add(i, _):
-            here = rows16(i)
-            z2_st[slot - 1, here] = (
-                ysum[slot, mine, here].astype(F32) + z1_in[slot, here].astype(F32)
-            ).astype(BF16)
-            return 0
-
-        lax.fori_loop(0, HALF // 16, add, 0)
-        send(("z2", slot), z2_st.at[slot - 1], z2_in.at[slot - 1], z_far[slot])
+        send(("zb", slot), ysum.at[slot, 1 - mine], zb_in.at[slot], z_other[slot])
+        if slot:
+            send(("za", slot), ysum.at[slot, mine], za_in.at[slot - 1], z_same[slot])
 
     def back(group):
         t = pl.ds(group * GROUP, GROUP)
@@ -248,60 +293,58 @@
         lax.fori_loop(0, TOK // 16, add, 0)
         send(("dx", group), dn_st.at[group - 1], dn_in.at[group - 1], peer)
 
+    pass_w1(0)
     pass_neighbours("u")
-    pass_w1(0)
+    pass_w1(1)
     recv(("u", "s0"), ("n", "s0"))
     forward(0, 0)
+    pass_w1(2)
+    pass_w3(0)
+    pass_w1(3)
     pass_neighbours("n")
-    pass_w1(1)
+    pass_w3(1)
     recv(("u", "s1"), ("n", "s1"))
     forward(0, 1)
-    pass_w3(0)
+    pass_w3(2)
     recv(("u", "s3"), ("n", "s3"))
     forward(0, 3)
-    pass_w1(2)
     pass_opposite("u")
+    pass_w3(3)
+    pass_opposite("n")
     pass_w2(0)
-    pass_opposite("n")
-    pass_w3(1)
     recv(("u", "s2"), ("n", "s2"))
     forward(0, 2)
-    pass_w1(3)
     pass_w2(1)
     grads(0)
     y1(0)
-    pass_w3(2)
+    all_w(1)
     forward_all(1)
-    pass_w2(2)
-    pass_w3(3)
+    pass_last()
     grads(1)
     y1(1)
-    y2(0)
-    pass_w2(3)
+    all_w(3)
     forward_all(3)
     grads(3)
     y1(3)
     y2(1)
-    recv(("w2", 0), ("w2", 1), ("w2", 2), ("w2", 3))
+    all_w(2)
     forward_all(2)
     grads(2)
     y1(2)
     y2(3)
-    y3(0)
     back(2)
+    y2(2)
+    y2(0)
+    y3(1)
     back(1)
-    y2(2)
     back(3)
     back(0)
     dn_pass(2, x_far)
     dn_pass(1, xr)
     dn_pass(3, xl)
-    y3(1)
     y3(3)
-    z2(1)
-    z2(3)
     y3(2)
-    z2(2)
+    y3(0)
 
     recv(("dn", 0), ("dx", 1), ("dx", 2), ("dx", 3))
 
@@ -321,14 +364,14 @@
 
     lax.fori_loop(0, TOK // 16, finish, 0)
 
-    recv(("z1", 0), ("z2", 1), ("z2", 2), ("z2", 3))
+    recv(*[("za", k) for k in (1, 2, 3)], *[("zb", k) for k in range(4)])
     total[:, pl.ds(WIN, 128)] = jnp.zeros((16, 128), F32)
 
     def split(i, _):
         here = rows16(i)
-        rows = ysum[0, mine, here].astype(F32) + z1_in[0, here].astype(F32)
+        rows = ysum[0, mine, here].astype(F32) + zb_in[0, here].astype(F32)
         for k in range(3):
-            rows += z2_in[k, here].astype(F32)
+            rows += za_in[k, here].astype(F32) + zb_in[k + 1, here].astype(F32)
         total[:, pl.ds(0, WIN)] = rows
         for q in range(4):
             turned = pltpu.roll(total[...], (WIN + 128 - 104 * q) - 32 * y, 1)
@@ -347,34 +390,34 @@
     lax.fori_loop(0, HALF // 16, keep, 0)
     recv(("f", "sib"), ("f", "in"), ("f", "cross"))
 
-    def store(i, _):
-        here = rows16(i)
-        for q in range(4):
-            out_ref[q, here] = fin_in[q, here].astype(F32)
-        return 0
-
-    lax.fori_loop(0, HALF // 16, store, 0)
-    for copy in copies.values():
-        copy.wait_send()
+    for q in range(2):
+        up_rows[pl.ds(q * HALF, HALF)] = fin_in[q].astype(F32)
+        rows = (HALF, 400 - HALF)[q]
+        down_out[pl.ds(q * HALF, rows), :] = fin_in[2 + q, pl.ds(0, rows)].astype(F32)[:, :104]
+    up_rows[pl.ds(2 * HALF, 96)] = jnp.zeros((96, 128), F32)
+    up_out[...] = up_rows[...].T[:104, :400]
+    for key, copy in copies.items():
+        if key in only:
+            pl.when(only[key])(copy.wait_send)
+        else:
+            copy.wait_send()
 
 
 def body(inputs, gain, w_up, w_down, upstream):
-    core = lax.axis_index("dp") % 2
-    up_rows = jnp.pad(w_up, ((0, 0), (0, 16)))
-    down_rows = jnp.pad(w_down, ((0, 16), (0, 0)))
-    w_own = jnp.stack([
-        lax.dynamic_slice_in_dim(up_rows, core * HALF, HALF, 1).T,
-        lax.dynamic_slice_in_dim(down_rows, core * HALF, HALF, 0),
-    ])
     vmem = pl.BlockSpec(memory_space=pltpu.VMEM)
-    input_grad, pieces = pl.pallas_call(
+    return pl.pallas_call(
         kernel,
-        out_shape=(jax.ShapeDtypeStruct((TOK, D), BF16), jax.ShapeDtypeStruct((4, HALF, 128), F32)),
-        in_specs=[vmem, vmem, vmem, pl.BlockSpec(memory_space=pl.ANY)],
-        out_specs=(vmem, vmem),
+        out_shape=(
+            jax.ShapeDtypeStruct((TOK, D), BF16),
+            jax.ShapeDtypeStruct((104, 400), F32),
+            jax.ShapeDtypeStruct((400, 104), F32),
+        ),
+        in_specs=[vmem] * 5,
+        out_specs=(vmem,) * 3,
         scratch_shapes=[
             pltpu.VMEM((T, D), BF16),
             pltpu.VMEM((T, D), BF16),
+            pltpu.VMEM((2 * HALF, D), BF16),
             pltpu.VMEM((2, HID, D), BF16),
             pltpu.VMEM((HID, T), BF16),
             pltpu.VMEM((HID, T), BF16),
@@ -383,28 +426,24 @@
             pltpu.VMEM((4, 2, 2, HALF, 256), BF16),
             pltpu.VMEM((4, 2, 2, HALF, WIN), BF16),
             pltpu.VMEM((4, 2, HALF, WIN), BF16),
+            pltpu.VMEM((3, HALF, WIN), BF16),
             pltpu.VMEM((4, HALF, WIN), BF16),
-            pltpu.VMEM((3, HALF, WIN), BF16),
-            pltpu.VMEM((3, HALF, WIN), BF16),
             pltpu.VMEM((16, WIN + 128), F32),
             pltpu.VMEM((4, HALF, 128), BF16),
             pltpu.VMEM((4, HALF, 128), BF16),
+            pltpu.VMEM((512, 128), F32),
             pltpu.VMEM((4, 2, TOK, D), BF16),
             pltpu.VMEM((4, TOK, D), BF16),
             pltpu.VMEM((3, TOK, D), BF16),
             pltpu.VMEM((3, TOK, D), BF16),
             pltpu.SemaphoreType.DMA((N_SEM,)),
             pltpu.SemaphoreType.DMA((N_SEM,)),
-            pltpu.SemaphoreType.DMA,
         ],
         compiler_params=pltpu.CompilerParams(
             collective_id=1, has_side_effects=True, vmem_limit_bytes=60 * 2**20
         ),
         name="block_backward",
-    )(inputs, upstream, gain.astype(F32).reshape(1, D), w_own)
-    up_grad = pieces[:2].reshape(2 * HALF, 128)[:400, :104].T
-    down_grad = pieces[2:].reshape(2 * HALF, 128)[:400, :104]
-    return input_grad, up_grad, down_grad
+    )(inputs, upstream, gain.astype(F32).reshape(1, D), w_up, w_down)
 
 
 def solution(mesh):

time: 155 us -> 155 us (level)
  local copies, waits for them, and re-layouts: 5.42 us -> 9.02 us
  Pallas kernels: 147 us -> 145 us
    unnamed x7 -> x5, local copies, waits for them, and re-layouts: 1.01 us -> 5.95 us
    pallas_call x1, Pallas kernels: 147 us -> 145 us  [body(): pl.pallas_call(kernel, out_shape=(jax.ShapeDtypeStruct((TOK, D), BF16), j...]
    slice x2 -> x0, local copies, waits for them, and re-layouts: 1.81 us -> none  [body(): down_grad = pieces[2:].reshape(2 * HALF, 128)[:400, :104]]
    pallas_call x0 -> x1, local copies, waits for them, and re-layouts: none -> 1.79 us  [body(): pl.pallas_call(kernel, out_shape=(jax.ShapeDtypeStruct((TOK, D), BF16), j...]
where the time goes in v2:
time: 155 us
  Pallas kernels  145 us (94%)
  local copies, waits for them, and re-layouts  9.02 us (6%)
    pallas_call x1, Pallas kernels, body(): pl.pallas_call(kernel, out_shape=(jax.ShapeDtypeStruct((TOK, D), BF16), j...  145 us
    unnamed x5, local copies, waits for them, and re-layouts  5.95 us

profile of v2, /device:TPU:1, one launch (start us, length us, event | category | flops | bytes accessed | tf_op | source)
XLA Modules:
  0.0 154.6 jit_solution(9849909744632043882)
XLA Ops:
  0.6 1.3 reshape.14.gain_ref
  1.9 3.5 %copy.8.wu_ref = bf16[1664,400]{1,0:T(8,128)(2,1)} copy(bf16[1664,400]{0,1:T(8,128)(2,1)} %param.7) | data formatting | bytes 2662400 | tf_op args[2]
  5.4 144.9 %block_backward.1 = (bf16[128,1664]{1,0:T(8,128)(2,1)}, f32[104,400]{1,0:T(8,128)}, f32[400,104]{1,0:T(8,128)}) custom-call(bf16[128,1664]{1,0:T(8,128)(2,1)} %x_ref.1, bf16[128,1664]{1,0:T(8,128)(2,1)} %up_ref.1, f32[1,1664]{1,0:T(1,128)} %reshape.14.gain_ref, bf16[1664,400]{1,0:T(8,128)(2,1)} %copy.8.wu_ref, bf16[400,1664]{1,0:T(8,128)(2,1)} %wd_ref.1), custom_call_target="tpu_custom_call" | custom-call | tf_op jit(solution)/shard_map/block_backward/pallas_call | solution.py:408
  150.3 0.0 copy-start
  150.3 1.8 %copy.9 = f32[104,400]{0,1:T(8,128)} copy(f32[104,400]{1,0:T(8,128)} %get-tuple-element.4) | data formatting | bytes 332800 | tf_op jit(solution)/shard_map/block_backward/pallas_call | solution.py:408
  152.1 1.8 %copy.12 = bf16[128,1664]{1,0:T(8,128)(2,1)} copy(bf16[128,1664]{1,0:T(8,128)(2,1)} %get-tuple-element.9) | data formatting | bytes 851968
  153.9 0.0 copy-done
  153.9 0.7 copy.13
Async XLA Ops:
  150.3 3.6 %copy-start = (f32[400,104]{1,0:T(8,128)S(1)}, f32[400,104]{1,0:T(8,128)}, u32[]{:S(2)}) copy-start(f32[400,104]{1,0:T(8,128)} %get-tuple-element.11) | copy-start | bytes 499204

commit v3 on v2

--- a/solution.py
+++ b/solution.py
@@ -34,7 +34,7 @@
 
 def kernel(
     x_ref, up_ref, gain_ref, wu_ref, wd_ref, grad_ref, up_out, down_out,
-    tok_n, tok_u, wt, w, hid, dpre, g, yo_in, ya_st, nb_in, ysum, za_in, zb_in, total, fin_st, fin_in, up_rows,
+    tok_n, tok_u, w, hid, dpre, g, yo_in, ya_st, nb_in, ysum, za_in, zb_in, pair_in, total, fin_st, fin_in,
     dn, dn_sib, dn_st, dn_in, ss, rs,
 ):
     dp, tensor = lax.axis_index("dp"), lax.axis_index("tensor")
@@ -47,14 +47,14 @@
     yr, yl = place(x, y + 1, z, c), place(x, y - 1, z, c)
     z_out, z_in = place(x, y, z + step_out, c), place(x, y, z - step_out, c)
     z_cross = place(x, y, z - step_out, 1 - c)
-    z_same = {1: place(x, y, z + 2 * step_out, c), 2: place(x, y, z + 4, c), 3: place(x, y, z - 2 * step_out, c)}
-    z_other = {0: z_in, 1: z_out, 2: place(x, y, z + 3 * step_out, c), 3: place(x, y, z - 3 * step_out, c)}
+    z_same = {1: place(x, y, z + 2 * step_out, c), 2: place(x, y, z + 4, c)}
+    z_other = {0: z_in, 1: z_out, 2: place(x, y, z + 3 * step_out, c)}
     kind = y % 2
     from_out, from_in = 16 + 96 * zl, 112 - 96 * zl
     mine = zl
 
     barrier = pltpu.get_barrier_semaphore()
-    peers = [sib, xr, xl, x_far, yr, yl, z_cross, *z_same.values(), *z_other.values()]
+    peers = [sib, xr, xl, x_far, yr, yl, z_cross, place(x, y, z - 2 * step_out, c), *z_same.values(), *z_other.values()]
     for peer in peers:
         pl.semaphore_signal(barrier, inc=1, device_id=peer, device_id_type=MESH)
 
@@ -99,20 +99,16 @@
     pl.semaphore_wait(barrier, len(peers))
     send_own("u")
 
-    for n in range(13):
-        cols = pl.ds(n * 128, 128)
-        wt[pl.ds(0, 400), cols] = wu_ref[cols, :].T
-    wt[pl.ds(400, 16)] = jnp.zeros((16, D), BF16)
-    w[0, pl.ds(0, HALF)] = wt[pl.ds(pl.multiple_of(c * HALF, 16), HALF)]
-
-    @pl.when(c == 0)
-    def _():
-        w[1, pl.ds(0, HALF)] = wd_ref[pl.ds(0, HALF)]
-
-    @pl.when(c == 1)
-    def _():
-        w[1, pl.ds(0, 192)] = wd_ref[pl.ds(HALF, 192)]
-        w[1, pl.ds(192, 16)] = jnp.zeros((16, D), BF16)
+    for k, ref in enumerate((wu_ref, wd_ref)):
+        w[k, pl.ds(0, 192)] = ref[pl.ds(pl.multiple_of(c * HALF, 16), 192)]
+
+        @pl.when(c == 0)
+        def _():
+            w[k, pl.ds(192, 16)] = ref[pl.ds(192, 16)]
+
+        @pl.when(c == 1)
+        def _():
+            w[k, pl.ds(192, 16)] = jnp.zeros((16, D), BF16)
 
     def rows_of(slot, first, rows):
         return pl.ds(pl.multiple_of(slot * HALF + first, 16), rows)
@@ -220,50 +216,78 @@
     def window(owner, first=0, cols=WIN):
         return pl.ds(pl.multiple_of(((owner + 8) % 4) * 384 + first, 128), cols)
 
-    def y1(slot):
-        r = pl.ds(slot * HALF, HALF)
-        send(("yo", slot, 0), g.at[:, r, window(y + 2, 0, 256)], yo_in.at[slot, 0], yr)
-        send(("yo", slot, 1), g.at[:, r, window(y + 2, 256, 256)], yo_in.at[slot, 1], yl)
-        send(("yd", slot, 0), g.at[:, r, window(y + 1, 256, 256)], nb_in.at[slot, 0, :, :, pl.ds(256, 256)], yr)
-        send(("yd", slot, 1), g.at[:, r, window(y - 1, 0, 256)], nb_in.at[slot, 1, :, :, pl.ds(0, 256)], yl)
-
     def rows16(i):
         return pl.ds(pl.multiple_of(i * 16, 16), 16)
 
-    def y2(slot):
+    def slot16(slot, i):
+        return pl.ds(pl.multiple_of(slot * HALF + i * 16, 16), 16)
+
+    def kinds(part):
+        return pl.ds(0, 2) if part[1] is None else pl.ds(part[1], 1)
+
+    def y1(*part):
+        r, k = pl.ds(part[0] * HALF, HALF), kinds(part)
+        left, right = pl.ds(0, 256), pl.ds(256, 256)
+        send(("yo", part, 0), g.at[k, r, window(y + 2, 0, 256)], yo_in.at[part[0], 0, k], yr)
+        send(("yo", part, 1), g.at[k, r, window(y + 2, 256, 256)], yo_in.at[part[0], 1, k], yl)
+        send(("yd", part, 0), g.at[k, r, window(y + 1, 256, 256)], nb_in.at[part[0], 0, k, :, right], yr)
+        send(("yd", part, 1), g.at[k, r, window(y - 1, 0, 256)], nb_in.at[part[0], 1, k, :, left], yl)
+
+    def y2(*part):
+        slot, k = part[0], kinds(part)
         for way, owner, first, peer in ((0, y + 1, 0, yr), (1, y - 1, 256, yl)):
-            recv(("yo", slot, way))
+            recv(("yo", part, way))
             cols = window(owner, first, 256)
 
             def add(i, _):
-                part = pl.ds(pl.multiple_of(slot * HALF + i * 16, 16), 16)
                 here = rows16(i)
-                ya_st[slot, way, :, here] = (
-                    g[:, part, cols].astype(F32) + yo_in[slot, way, :, here].astype(F32)
+                ya_st[slot, way, k, here] = (
+                    g[k, slot16(slot, i), cols].astype(F32) + yo_in[slot, way, k, here].astype(F32)
                 ).astype(BF16)
                 return 0
 
             lax.fori_loop(0, HALF // 16, add, 0)
-            send(("ya", slot, way), ya_st.at[slot, way], nb_in.at[slot, way, :, :, pl.ds(first, 256)], peer)
-
-    def y3(slot):
-        recv(("yd", slot, 0), ("yd", slot, 1), ("ya", slot, 0), ("ya", slot, 1))
+            send(("ya", part, way), ya_st.at[slot, way, k], nb_in.at[slot, way, k, :, pl.ds(first, 256)], peer)
+
+    def y3(*part):
+        slot, k = part[0], kinds(part)
+        recv(("yd", part, 0), ("yd", part, 1), ("ya", part, 0), ("ya", part, 1))
         cols = window(y)
 
         def add(i, _):
-            part = pl.ds(pl.multiple_of(slot * HALF + i * 16, 16), 16)
             here = rows16(i)
-            ysum[slot, :, here] = (
-                g[:, part, cols].astype(F32)
-                + nb_in[slot, 0, :, here].astype(F32)
-                + nb_in[slot, 1, :, here].astype(F32)
+            ysum[slot, k, here] = (
+                g[k, slot16(slot, i), cols].astype(F32)
+                + nb_in[slot, 0, k, here].astype(F32)
+                + nb_in[slot, 1, k, here].astype(F32)
             ).astype(BF16)
             return 0
 
         lax.fori_loop(0, HALF // 16, add, 0)
-        send(("zb", slot), ysum.at[slot, 1 - mine], zb_in.at[slot], z_other[slot])
-        if slot:
-            send(("za", slot), ysum.at[slot, mine], za_in.at[slot - 1], z_same[slot])
+        if part[1] in (None, 0):
+            make(("zb", slot), ysum.at[slot, 1 - mine], zb_in.at[slot], z_other[slot])
+            if slot:
+                make(("za", slot), ysum.at[slot, mine], za_in.at[slot - 1], z_same[slot])
+        if part[1] is None:
+            for key in ("zb", "za")[: 1 + (slot > 0)]:
+                start((key, slot))
+        else:
+            pl.when(mine == part[1])(copies["za", slot].start)
+            pl.when(mine != part[1])(copies["zb", slot].start)
+
+    def pair_send():
+        for k in range(2):
+            send(("pair", k), g.at[k, pl.ds(3 * HALF, HALF)], pair_in.at[k], z_in)
+
+    def pair_add(k):
+        recv(("pair", k))
+
+        def add(i, _):
+            here = slot16(1, i)
+            g[k, here] = (g[k, here].astype(F32) + pair_in[k, rows16(i)].astype(F32)).astype(BF16)
+            return 0
+
+        lax.fori_loop(0, HALF // 16, add, 0)
 
     def back(group):
         t = pl.ds(group * GROUP, GROUP)
@@ -308,43 +332,46 @@
     pass_w3(2)
     recv(("u", "s3"), ("n", "s3"))
     forward(0, 3)
+    pass_w3(3)
     pass_opposite("u")
-    pass_w3(3)
     pass_opposite("n")
     pass_w2(0)
     recv(("u", "s2"), ("n", "s2"))
     forward(0, 2)
+    grads(0)
+    y1(0, None)
     pass_w2(1)
-    grads(0)
-    y1(0)
-    all_w(1)
-    forward_all(1)
-    pass_last()
-    grads(1)
-    y1(1)
     all_w(3)
     forward_all(3)
+    pass_last()
     grads(3)
-    y1(3)
-    y2(1)
+    pair_send()
+    y2(0, None)
     all_w(2)
     forward_all(2)
     grads(2)
-    y1(2)
-    y2(3)
+    y1(2, None)
+    all_w(1)
+    forward_all(1)
+    grads(1)
+    y2(2, None)
+    y3(0, None)
     back(2)
-    y2(2)
-    y2(0)
-    y3(1)
+    pair_add(0)
+    y1(1, 0)
     back(1)
+    y2(1, 0)
     back(3)
+    pair_add(1)
+    y1(1, 1)
+    y3(2, None)
     back(0)
+    y2(1, 1)
     dn_pass(2, x_far)
     dn_pass(1, xr)
     dn_pass(3, xl)
-    y3(3)
-    y3(2)
-    y3(0)
+    y3(1, 0)
+    y3(1, 1)
 
     recv(("dn", 0), ("dx", 1), ("dx", 2), ("dx", 3))
 
@@ -364,13 +391,13 @@
 
     lax.fori_loop(0, TOK // 16, finish, 0)
 
-    recv(*[("za", k) for k in (1, 2, 3)], *[("zb", k) for k in range(4)])
+    recv(*[("za", k) for k in (1, 2)], *[("zb", k) for k in range(3)])
     total[:, pl.ds(WIN, 128)] = jnp.zeros((16, 128), F32)
 
     def split(i, _):
         here = rows16(i)
         rows = ysum[0, mine, here].astype(F32) + zb_in[0, here].astype(F32)
-        for k in range(3):
+        for k in range(2):
             rows += za_in[k, here].astype(F32) + zb_in[k + 1, here].astype(F32)
         total[:, pl.ds(0, WIN)] = rows
         for q in range(4):
@@ -391,11 +418,9 @@
     recv(("f", "sib"), ("f", "in"), ("f", "cross"))
 
     for q in range(2):
-        up_rows[pl.ds(q * HALF, HALF)] = fin_in[q].astype(F32)
         rows = (HALF, 400 - HALF)[q]
+        up_out[pl.ds(q * HALF, rows), :] = fin_in[q, pl.ds(0, rows)].astype(F32)[:, :104]
         down_out[pl.ds(q * HALF, rows), :] = fin_in[2 + q, pl.ds(0, rows)].astype(F32)[:, :104]
-    up_rows[pl.ds(2 * HALF, 96)] = jnp.zeros((96, 128), F32)
-    up_out[...] = up_rows[...].T[:104, :400]
     for key, copy in copies.items():
         if key in only:
             pl.when(only[key])(copy.wait_send)
@@ -405,11 +430,11 @@
 
 def body(inputs, gain, w_up, w_down, upstream):
     vmem = pl.BlockSpec(memory_space=pltpu.VMEM)
-    return pl.pallas_call(
+    input_grad, up_grad, down_grad = pl.pallas_call(
         kernel,
         out_shape=(
             jax.ShapeDtypeStruct((TOK, D), BF16),
-            jax.ShapeDtypeStruct((104, 400), F32),
+            jax.ShapeDtypeStruct((400, 104), F32),
             jax.ShapeDtypeStruct((400, 104), F32),
         ),
         in_specs=[vmem] * 5,
@@ -417,21 +442,20 @@
         scratch_shapes=[
             pltpu.VMEM((T, D), BF16),
             pltpu.VMEM((T, D), BF16),
-            pltpu.VMEM((2 * HALF, D), BF16),
             pltpu.VMEM((2, HID, D), BF16),
             pltpu.VMEM((HID, T), BF16),
             pltpu.VMEM((HID, T), BF16),
             pltpu.VMEM((2, HID, D), BF16),
-            pltpu.VMEM((4, 2, 2, HALF, 256), BF16),
-            pltpu.VMEM((4, 2, 2, HALF, 256), BF16),
-            pltpu.VMEM((4, 2, 2, HALF, WIN), BF16),
-            pltpu.VMEM((4, 2, HALF, WIN), BF16),
+            pltpu.VMEM((3, 2, 2, HALF, 256), BF16),
+            pltpu.VMEM((3, 2, 2, HALF, 256), BF16),
+            pltpu.VMEM((3, 2, 2, HALF, WIN), BF16),
+            pltpu.VMEM((3, 2, HALF, WIN), BF16),
+            pltpu.VMEM((2, HALF, WIN), BF16),
             pltpu.VMEM((3, HALF, WIN), BF16),
-            pltpu.VMEM((4, HALF, WIN), BF16),
+            pltpu.VMEM((2, HALF, D), BF16),
             pltpu.VMEM((16, WIN + 128), F32),
             pltpu.VMEM((4, HALF, 128), BF16),
             pltpu.VMEM((4, HALF, 128), BF16),
-            pltpu.VMEM((512, 128), F32),
             pltpu.VMEM((4, 2, TOK, D), BF16),
             pltpu.VMEM((4, TOK, D), BF16),
             pltpu.VMEM((3, TOK, D), BF16),
@@ -443,7 +467,8 @@
             collective_id=1, has_side_effects=True, vmem_limit_bytes=60 * 2**20
         ),
         name="block_backward",
-    )(inputs, upstream, gain.astype(F32).reshape(1, D), w_up, w_down)
+    )(inputs, upstream, gain.astype(F32).reshape(1, D), w_up.T, w_down)
+    return input_grad, up_grad.T, down_grad
 
 
 def solution(mesh):

time: 155 us -> 136 us (0.88)
  Pallas kernels: 145 us -> 130 us
  local copies, waits for them, and re-layouts: 9.02 us -> 5.43 us
    pallas_call x1, Pallas kernels: 145 us -> 130 us  [body(): pl.pallas_call(kernel, out_shape=(jax.ShapeDtypeStruct((TOK, D), BF16), j...]
    unnamed x5, local copies, waits for them, and re-layouts: 5.95 us -> 4.14 us
    pallas_call x1 -> x0, local copies, waits for them, and re-layouts: 1.79 us -> none  [body(): pl.pallas_call(kernel, out_shape=(jax.ShapeDtypeStruct((TOK, D), BF16), j...]
where the time goes in v3:
time: 136 us
  Pallas kernels  130 us (96%)
  local copies, waits for them, and re-layouts  5.43 us (4%)
    pallas_call x1, Pallas kernels, body(): pl.pallas_call(kernel, out_shape=(jax.ShapeDtypeStruct((TOK, D), BF16), j...  130 us
    unnamed x5, local copies, waits for them, and re-layouts  4.14 us

profile of v3, /device:TPU:1, one launch (start us, length us, event | category | flops | bytes accessed | tf_op | source)
XLA Modules:
  0.0 135.8 jit_solution(6419827354890159459)
XLA Ops:
  0.6 1.3 reshape.14.gain_ref
  1.9 129.7 %block_backward.1 = (bf16[128,1664]{1,0:T(8,128)(2,1)}, f32[400,104]{1,0:T(8,128)}, f32[400,104]{1,0:T(8,128)}) custom-call(bf16[128,1664]{1,0:T(8,128)(2,1)} %x_ref.1, bf16[128,1664]{1,0:T(8,128)(2,1)} %up_ref.1, f32[1,1664]{1,0:T(1,128)} %reshape.14.gain_ref, bf16[400,1664]{1,0:T(8,128)(2,1)} %bitcast.2, bf16[400,1664]{1,0:T(8,128)(2,1)} %wd_ref.1), custom_call_target="tpu_custom_call" | custom-call | tf_op jit(solution)/shard_map/block_backward/pallas_call | solution.py:433
  131.6 0.0 copy-start
  131.7 1.8 %copy.11 = bf16[128,1664]{1,0:T(8,128)(2,1)} copy(bf16[128,1664]{1,0:T(8,128)(2,1)} %get-tuple-element.12) | data formatting | bytes 851968
  133.5 1.6 %copy.12 = f32[104,400]{0,1:T(8,128)} copy(f32[104,400]{0,1:T(8,128)} %bitcast.3) | data formatting | bytes 332800
  135.1 0.0 copy-done
  135.1 0.7 copy.13
Async XLA Ops:
  131.6 3.5 %copy-start = (f32[400,104]{1,0:T(8,128)S(1)}, f32[400,104]{1,0:T(8,128)}, u32[]{:S(2)}) copy-start(f32[400,104]{1,0:T(8,128)} %get-tuple-element.14) | copy-start | bytes 499204

commit v4 on v3

--- a/solution.py
+++ b/solution.py
@@ -17,7 +17,7 @@
 HID = 4 * HALF
 WIN = 512
 CHUNKS = ((0, 64), (64, 48), (112, 48), (160, 48))
-N_SEM = 88
+N_SEM = 96
 GRAD_SCALE = float(32768) ** (-0.5)
 
 
@@ -34,7 +34,7 @@
 
 def kernel(
     x_ref, up_ref, gain_ref, wu_ref, wd_ref, grad_ref, up_out, down_out,
-    tok_n, tok_u, w, hid, dpre, g, yo_in, ya_st, nb_in, ysum, za_in, zb_in, pair_in, total, fin_st, fin_in,
+    tok_n, tok_u, w, hid, dpre, g, yo_in, ya_st, nb_in, ysum, z_sum, pair_in, total, fin_st, fin_in,
     dn, dn_sib, dn_st, dn_in, ss, rs,
 ):
     dp, tensor = lax.axis_index("dp"), lax.axis_index("tensor")
@@ -47,14 +47,14 @@
     yr, yl = place(x, y + 1, z, c), place(x, y - 1, z, c)
     z_out, z_in = place(x, y, z + step_out, c), place(x, y, z - step_out, c)
     z_cross = place(x, y, z - step_out, 1 - c)
-    z_same = {1: place(x, y, z + 2 * step_out, c), 2: place(x, y, z + 4, c)}
-    z_other = {0: z_in, 1: z_out, 2: place(x, y, z + 3 * step_out, c)}
+    z_same = {1: place(x, y, z + 2 * step_out, c), 2: place(x, y, z + 4, c), 3: place(x, y, z - 2 * step_out, c)}
+    z_other = {0: z_in, 1: z_out, 2: place(x, y, z + 3 * step_out, c), 3: place(x, y, z - 3 * step_out, c)}
     kind = y % 2
     from_out, from_in = 16 + 96 * zl, 112 - 96 * zl
     mine = zl
 
     barrier = pltpu.get_barrier_semaphore()
-    peers = [sib, xr, xl, x_far, yr, yl, z_cross, place(x, y, z - 2 * step_out, c), *z_same.values(), *z_other.values()]
+    peers = [sib, xr, xl, x_far, yr, yl, z_cross, *z_same.values(), *z_other.values()]
     for peer in peers:
         pl.semaphore_signal(barrier, inc=1, device_id=peer, device_id_type=MESH)
 
@@ -190,12 +190,12 @@
         hid[r, t] = hidden.astype(BF16)
         dpre[r, t] = (dhidden * slope).astype(BF16)
 
-    def forward_all(slot):
+    def forward_all(slot, first=0):
         def one(group, _):
             forward(slot, group)
             return 0
 
-        lax.fori_loop(0, 4, one, 0)
+        lax.fori_loop(first, 4, one, 0)
 
     def grads(slot):
         r = pl.ds(slot * HALF, HALF)
@@ -264,26 +264,25 @@
             return 0
 
         lax.fori_loop(0, HALF // 16, add, 0)
-        if part[1] in (None, 0):
-            make(("zb", slot), ysum.at[slot, 1 - mine], zb_in.at[slot], z_other[slot])
-            if slot:
-                make(("za", slot), ysum.at[slot, mine], za_in.at[slot - 1], z_same[slot])
-        if part[1] is None:
-            for key in ("zb", "za")[: 1 + (slot > 0)]:
-                start((key, slot))
+        if slot == 2:
+            send(("zb", 2), ysum.at[2, 1 - mine], z_sum.at[1], z_other[2])
+            send(("za", 2), ysum.at[2, mine], z_sum.at[2], z_same[2])
+        elif slot == 0:
+            if ("zb", 0) not in copies:
+                make(("zb", 0), ysum.at[0, 1 - mine], z_sum.at[0], z_other[0])
+            pl.when(mine != part[1])(copies["zb", 0].start)
         else:
-            pl.when(mine == part[1])(copies["za", slot].start)
-            pl.when(mine != part[1])(copies["zb", slot].start)
-
-    def pair_send():
-        for k in range(2):
-            send(("pair", k), g.at[k, pl.ds(3 * HALF, HALF)], pair_in.at[k], z_in)
+            send(("zb", slot), ysum.at[slot, part[1]], z_sum.at[3], z_other[slot], mine != part[1])
+            send(("za", slot), ysum.at[slot, part[1]], z_sum.at[4], z_same[slot], mine == part[1])
+
+    def pair_send(k):
+        send(("pair", k), g.at[k, pl.ds((3, 1)[k] * HALF, HALF)], pair_in.at[k], (z_in, z_out)[k])
 
     def pair_add(k):
         recv(("pair", k))
 
         def add(i, _):
-            here = slot16(1, i)
+            here = slot16((1, 0)[k], i)
             g[k, here] = (g[k, here].astype(F32) + pair_in[k, rows16(i)].astype(F32)).astype(BF16)
             return 0
 
@@ -335,43 +334,48 @@
     pass_w3(3)
     pass_opposite("u")
     pass_opposite("n")
-    pass_w2(0)
+    all_w(1)
+    forward(1, 0)
     recv(("u", "s2"), ("n", "s2"))
     forward(0, 2)
     grads(0)
-    y1(0, None)
+    y1(0, 0)
+    pass_w2(0)
+    forward_all(1, 1)
+    grads(1)
+    pair_send(1)
     pass_w2(1)
     all_w(3)
     forward_all(3)
+    grads(3)
+    pair_send(0)
+    y1(3, 1)
     pass_last()
-    grads(3)
-    pair_send()
-    y2(0, None)
+    y2(0, 0)
     all_w(2)
     forward_all(2)
     grads(2)
     y1(2, None)
-    all_w(1)
-    forward_all(1)
-    grads(1)
+    y2(3, 1)
+    y3(0, 0)
+    back(2)
+    pair_add(1)
+    y1(0, 1)
+    back(1)
     y2(2, None)
-    y3(0, None)
-    back(2)
     pair_add(0)
     y1(1, 0)
-    back(1)
+    y3(3, 1)
+    back(3)
+    y2(0, 1)
+    back(0)
     y2(1, 0)
-    back(3)
-    pair_add(1)
-    y1(1, 1)
     y3(2, None)
-    back(0)
-    y2(1, 1)
     dn_pass(2, x_far)
     dn_pass(1, xr)
     dn_pass(3, xl)
+    y3(0, 1)
     y3(1, 0)
-    y3(1, 1)
 
     recv(("dn", 0), ("dx", 1), ("dx", 2), ("dx", 3))
 
@@ -391,14 +395,16 @@
 
     lax.fori_loop(0, TOK // 16, finish, 0)
 
-    recv(*[("za", k) for k in (1, 2)], *[("zb", k) for k in range(3)])
+    recv(("zb", 0), ("zb", 2), ("za", 2))
+    recv(("zb", 1), ("za", 1), when=mine == 0)
+    recv(("zb", 3), ("za", 3), when=mine == 1)
     total[:, pl.ds(WIN, 128)] = jnp.zeros((16, 128), F32)
 
     def split(i, _):
         here = rows16(i)
-        rows = ysum[0, mine, here].astype(F32) + zb_in[0, here].astype(F32)
-        for k in range(2):
-            rows += za_in[k, here].astype(F32) + zb_in[k + 1, here].astype(F32)
+        rows = ysum[0, mine, here].astype(F32)
+        for k in range(5):
+            rows += z_sum[k, here].astype(F32)
         total[:, pl.ds(0, WIN)] = rows
         for q in range(4):
             turned = pltpu.roll(total[...], (WIN + 128 - 104 * q) - 32 * y, 1)
@@ -446,12 +452,11 @@
             pltpu.VMEM((HID, T), BF16),
             pltpu.VMEM((HID, T), BF16),
             pltpu.VMEM((2, HID, D), BF16),
-            pltpu.VMEM((3, 2, 2, HALF, 256), BF16),
-            pltpu.VMEM((3, 2, 2, HALF, 256), BF16),
-            pltpu.VMEM((3, 2, 2, HALF, WIN), BF16),
-            pltpu.VMEM((3, 2, HALF, WIN), BF16),
-            pltpu.VMEM((2, HALF, WIN), BF16),
-            pltpu.VMEM((3, HALF, WIN), BF16),
+            pltpu.VMEM((4, 2, 2, HALF, 256), BF16),
+            pltpu.VMEM((4, 2, 2, HALF, 256), BF16),
+            pltpu.VMEM((4, 2, 2, HALF, WIN), BF16),
+            pltpu.VMEM((4, 2, HALF, WIN), BF16),
+            pltpu.VMEM((5, HALF, WIN), BF16),
             pltpu.VMEM((2, HALF, D), BF16),
             pltpu.VMEM((16, WIN + 128), F32),
             pltpu.VMEM((4, HALF, 128), BF16),

time: 136 us -> 141 us (1.037)
  Pallas kernels: 130 us -> 135 us
    pallas_call x1, Pallas kernels: 130 us -> 135 us  [body(): pl.pallas_call(kernel, out_shape=(jax.ShapeDtypeStruct((TOK, D), BF16), j...]
where the time goes in v4:
time: 141 us
  Pallas kernels  135 us (96%)
  local copies, waits for them, and re-layouts  5.43 us (4%)
    pallas_call x1, Pallas kernels, body(): pl.pallas_call(kernel, out_shape=(jax.ShapeDtypeStruct((TOK, D), BF16), j...  135 us
    unnamed x5, local copies, waits for them, and re-layouts  4.14 us

profile of v4, /device:TPU:1, one launch (start us, length us, event | category | flops | bytes accessed | tf_op | source)
XLA Modules:
  0.0 140.6 jit_solution(17007354631589938300)
XLA Ops:
  0.6 1.3 reshape.14.gain_ref
  1.9 134.5 %block_backward.1 = (bf16[128,1664]{1,0:T(8,128)(2,1)}, f32[400,104]{1,0:T(8,128)}, f32[400,104]{1,0:T(8,128)}) custom-call(bf16[128,1664]{1,0:T(8,128)(2,1)} %x_ref.1, bf16[128,1664]{1,0:T(8,128)(2,1)} %up_ref.1, f32[1,1664]{1,0:T(1,128)} %reshape.14.gain_ref, bf16[400,1664]{1,0:T(8,128)(2,1)} %bitcast.2, bf16[400,1664]{1,0:T(8,128)(2,1)} %wd_ref.1), custom_call_target="tpu_custom_call" | custom-call | tf_op jit(solution)/shard_map/block_backward/pallas_call | solution.py:439
  136.5 0.0 copy-start
  136.5 1.8 %copy.11 = bf16[128,1664]{1,0:T(8,128)(2,1)} copy(bf16[128,1664]{1,0:T(8,128)(2,1)} %get-tuple-element.12) | data formatting | bytes 851968
  138.3 1.6 %copy.12 = f32[104,400]{0,1:T(8,128)} copy(f32[104,400]{0,1:T(8,128)} %bitcast.3) | data formatting | bytes 332800
  139.9 0.0 copy-done
  139.9 0.7 copy.13
Async XLA Ops:
  136.5 3.5 %copy-start = (f32[400,104]{1,0:T(8,128)S(1)}, f32[400,104]{1,0:T(8,128)}, u32[]{:S(2)}) copy-start(f32[400,104]{1,0:T(8,128)} %get-tuple-element.14) | copy-start | bytes 499204

commit v5 on v4

--- a/solution.py
+++ b/solution.py
@@ -19,6 +19,8 @@
 CHUNKS = ((0, 64), (64, 48), (112, 48), (160, 48))
 N_SEM = 96
 GRAD_SCALE = float(32768) ** (-0.5)
+
+FIRST = (0, HALF, 3 * HALF, 2 * HALF)
 
 
 def gelu_parts(pre):
@@ -87,6 +89,7 @@
     def tok_rows(group, core, first=0, rows=TOK):
         return pl.ds(pl.multiple_of(group * GROUP + core * TOK + first, 16), rows)
 
+    gain = gain_ref[...].astype(F32).reshape(1, D)
     own = tok_rows(0, c)
     tok_u[own] = up_ref[...]
     toks = {"u": tok_u, "n": tok_n}
@@ -111,7 +114,7 @@
             w[k, pl.ds(192, 16)] = jnp.zeros((16, D), BF16)
 
     def rows_of(slot, first, rows):
-        return pl.ds(pl.multiple_of(slot * HALF + first, 16), rows)
+        return pl.ds(pl.multiple_of(FIRST[slot] + first, 16), rows)
 
     def chunk(slot, i):
         return rows_of(slot, *CHUNKS[i])
@@ -123,7 +126,7 @@
         r = pl.ds(pl.multiple_of(i * 16, 16), 16)
         wide = x_ref[r].astype(F32)
         inv = lax.rsqrt(jnp.mean(wide * wide, axis=-1, keepdims=True) + norm_eps)
-        tok_n[tok_rows(0, c, i * 16, 16)] = (wide * inv * gain_ref[...]).astype(BF16)
+        tok_n[tok_rows(0, c, i * 16, 16)] = (wide * inv * gain).astype(BF16)
         return 0
 
     lax.fori_loop(0, TOK // 16, norm, 0)
@@ -180,9 +183,7 @@
     def all_w(slot):
         recv(*[key for key in copies if key[0] == "wy" and key[1][0] == slot])
 
-    def forward(slot, group):
-        r = pl.ds(slot * HALF, HALF)
-        t = pl.ds(pl.multiple_of(group * GROUP, GROUP), GROUP)
+    def forward(r, t):
         nt = (((1,), (1,)), ((), ()))
         pre = lax.dot_general(w[0, r], tok_n[t], nt, preferred_element_type=F32)
         dhidden = lax.dot_general(w[1, r], tok_u[t], nt, preferred_element_type=F32)
@@ -190,15 +191,18 @@
         hid[r, t] = hidden.astype(BF16)
         dpre[r, t] = (dhidden * slope).astype(BF16)
 
-    def forward_all(slot, first=0):
-        def one(group, _):
-            forward(slot, group)
-            return 0
-
-        lax.fori_loop(first, 4, one, 0)
-
-    def grads(slot):
-        r = pl.ds(slot * HALF, HALF)
+    def forward_one(slot, group):
+        forward(pl.ds(FIRST[slot], HALF), pl.ds(group * GROUP, GROUP))
+
+    def forward_all(slot, slots=1):
+        def one(i, _):
+            forward(pl.ds(FIRST[slot], slots * HALF), pl.ds(pl.multiple_of(i * 512, 512), 512))
+            return 0
+
+        lax.fori_loop(0, 2, one, 0)
+
+    def grads(slot, slots=1):
+        r = pl.ds(FIRST[slot], slots * HALF)
 
         def columns(cols):
             up = jnp.dot(dpre[r], tok_n[:, cols], preferred_element_type=F32)
@@ -207,10 +211,10 @@
             g[1, r, cols] = (down * GRAD_SCALE).astype(BF16)
 
         def tile(n, _):
-            columns(pl.ds(pl.multiple_of(n * 256, 256), 256))
-            return 0
-
-        lax.fori_loop(0, 6, tile, 0)
+            columns(pl.ds(pl.multiple_of(n * 512, 512), 512))
+            return 0
+
+        lax.fori_loop(0, 3, tile, 0)
         columns(pl.ds(1536, 128))
 
     def window(owner, first=0, cols=WIN):
@@ -220,13 +224,13 @@
         return pl.ds(pl.multiple_of(i * 16, 16), 16)
 
     def slot16(slot, i):
-        return pl.ds(pl.multiple_of(slot * HALF + i * 16, 16), 16)
+        return pl.ds(pl.multiple_of(FIRST[slot] + i * 16, 16), 16)
 
     def kinds(part):
         return pl.ds(0, 2) if part[1] is None else pl.ds(part[1], 1)
 
     def y1(*part):
-        r, k = pl.ds(part[0] * HALF, HALF), kinds(part)
+        r, k = pl.ds(FIRST[part[0]], HALF), kinds(part)
         left, right = pl.ds(0, 256), pl.ds(256, 256)
         send(("yo", part, 0), g.at[k, r, window(y + 2, 0, 256)], yo_in.at[part[0], 0, k], yr)
         send(("yo", part, 1), g.at[k, r, window(y + 2, 256, 256)], yo_in.at[part[0], 1, k], yl)
@@ -276,7 +280,7 @@
             send(("za", slot), ysum.at[slot, part[1]], z_sum.at[4], z_same[slot], mine == part[1])
 
     def pair_send(k):
-        send(("pair", k), g.at[k, pl.ds((3, 1)[k] * HALF, HALF)], pair_in.at[k], (z_in, z_out)[k])
+        send(("pair", k), g.at[k, pl.ds(FIRST[(3, 1)[k]], HALF)], pair_in.at[k], (z_in, z_out)[k])
 
     def pair_add(k):
         recv(("pair", k))
@@ -298,10 +302,10 @@
             dn[group, 1, :, cols] = part[TOK:]
 
         def tile(n, _):
-            columns(pl.ds(pl.multiple_of(n * 256, 256), 256))
-            return 0
-
-        lax.fori_loop(0, 6, tile, 0)
+            columns(pl.ds(pl.multiple_of(n * 512, 512), 512))
+            return 0
+
+        lax.fori_loop(0, 3, tile, 0)
         columns(pl.ds(1536, 128))
         send(("dn", group), dn.at[group, 1 - c], dn_sib.at[group], sib)
 
@@ -320,38 +324,35 @@
     pass_neighbours("u")
     pass_w1(1)
     recv(("u", "s0"), ("n", "s0"))
-    forward(0, 0)
+    forward_one(0, 0)
     pass_w1(2)
     pass_w3(0)
     pass_w1(3)
     pass_neighbours("n")
     pass_w3(1)
+    pass_w3(2)
     recv(("u", "s1"), ("n", "s1"))
-    forward(0, 1)
-    pass_w3(2)
-    recv(("u", "s3"), ("n", "s3"))
-    forward(0, 3)
+    forward_one(0, 1)
     pass_w3(3)
     pass_opposite("u")
+    recv(("u", "s3"), ("n", "s3"))
+    forward_one(0, 3)
+    pass_w2(0)
     pass_opposite("n")
-    all_w(1)
-    forward(1, 0)
     recv(("u", "s2"), ("n", "s2"))
-    forward(0, 2)
+    forward_one(0, 2)
+    pass_w2(1)
     grads(0)
     y1(0, 0)
-    pass_w2(0)
-    forward_all(1, 1)
-    grads(1)
+    pass_last()
+    all_w(1)
+    all_w(3)
+    forward_all(1, 2)
+    y2(0, 0)
+    grads(1, 2)
     pair_send(1)
-    pass_w2(1)
-    all_w(3)
-    forward_all(3)
-    grads(3)
     pair_send(0)
     y1(3, 1)
-    pass_last()
-    y2(0, 0)
     all_w(2)
     forward_all(2)
     grads(2)
@@ -359,21 +360,21 @@
     y2(3, 1)
     y3(0, 0)
     back(2)
+    back(1)
+    dn_pass(2, x_far)
+    y2(2, None)
     pair_add(1)
     y1(0, 1)
-    back(1)
-    y2(2, None)
+    back(3)
+    dn_pass(1, xr)
     pair_add(0)
     y1(1, 0)
+    back(0)
     y3(3, 1)
-    back(3)
+    dn_pass(3, xl)
     y2(0, 1)
-    back(0)
+    y3(2, None)
     y2(1, 0)
-    y3(2, None)
-    dn_pass(2, x_far)
-    dn_pass(1, xr)
-    dn_pass(3, xl)
     y3(0, 1)
     y3(1, 0)
 
@@ -381,7 +382,6 @@
 
     def finish(i, _):
         here = rows16(i)
-        gain = gain_ref[...]
         wide = x_ref[here].astype(F32)
         inv = lax.rsqrt(jnp.mean(wide * wide, axis=-1, keepdims=True) + norm_eps)
         unit = wide * inv
@@ -472,7 +472,7 @@
             collective_id=1, has_side_effects=True, vmem_limit_bytes=60 * 2**20
         ),
         name="block_backward",
-    )(inputs, upstream, gain.astype(F32).reshape(1, D), w_up.T, w_down)
+    )(inputs, upstream, gain, w_up.T, w_down)
     return input_grad, up_grad.T, down_grad
 
 

time: 141 us -> 123 us (0.87)
  Pallas kernels: 135 us -> 118 us
    pallas_call x1, Pallas kernels: 135 us -> 118 us  [body(): pl.pallas_call(kernel, out_shape=(jax.ShapeDtypeStruct((TOK, D), BF16), j...]
where the time goes in v5:
time: 123 us; the launch traced here: 122 us
  Pallas kernels  118 us (96%)
  local copies, waits for them, and re-layouts  4.14 us (3%)
    pallas_call x1, Pallas kernels, body(): pl.pallas_call(kernel, out_shape=(jax.ShapeDtypeStruct((TOK, D), BF16), j...  118 us
    unnamed x5, local copies, waits for them, and re-layouts  4.14 us

profile of v5, /device:TPU:1, one launch (start us, length us, event | category | flops | bytes accessed | tf_op | source)
XLA Modules:
  0.0 122.4 jit_solution(8056736320589624195)
XLA Ops:
  0.6 117.6 %block_backward.1 = (bf16[128,1664]{1,0:T(8,128)(2,1)}, f32[400,104]{1,0:T(8,128)}, f32[400,104]{1,0:T(8,128)}) custom-call(bf16[128,1664]{1,0:T(8,128)(2,1)} %x_ref.1, bf16[128,1664]{1,0:T(8,128)(2,1)} %up_ref.1, bf16[1664]{0:T(1024)(128)(2,1)} %gain_ref.1, bf16[400,1664]{1,0:T(8,128)(2,1)} %bitcast.2, bf16[400,1664]{1,0:T(8,128)(2,1)} %wd_ref.1), custom_call_target="tpu_custom_call" | custom-call | tf_op jit(solution)/shard_map/block_backward/pallas_call | solution.py:439
  118.2 0.0 copy-start
  118.2 1.8 %copy.11 = bf16[128,1664]{1,0:T(8,128)(2,1)} copy(bf16[128,1664]{1,0:T(8,128)(2,1)} %get-tuple-element.12) | data formatting | bytes 851968
  120.1 1.6 %copy.12 = f32[104,400]{0,1:T(8,128)} copy(f32[104,400]{0,1:T(8,128)} %bitcast.3) | data formatting | bytes 332800
  121.7 0.0 copy-done
  121.7 0.7 copy.13
Async XLA Ops:
  118.2 3.5 %copy-start = (f32[400,104]{1,0:T(8,128)S(1)}, f32[400,104]{1,0:T(8,128)}, u32[]{:S(2)}) copy-start(f32[400,104]{1,0:T(8,128)} %get-tuple-element.14) | copy-start | bytes 499204

commit v6 on v5

--- a/solution.py
+++ b/solution.py
@@ -6,6 +6,7 @@
 from jax.sharding import PartitionSpec as P
 
 MESH = pl.DeviceIdType.MESH
+PRE = ("outer", "inner", "swap")
 F32, BF16 = jnp.float32, jnp.bfloat16
 
 norm_eps = 1e-06
@@ -16,8 +17,9 @@
 HALF = 208
 HID = 4 * HALF
 WIN = 512
-CHUNKS = ((0, 64), (64, 48), (112, 48), (160, 48))
+CHUNKS = ((0, 64), (112, 48), (64, 48), (160, 48))
 N_SEM = 96
+RIGHT, LEFT, OPPOSITE = 1, 2, 3
 GRAD_SCALE = float(32768) ** (-0.5)
 
 FIRST = (0, HALF, 3 * HALF, 2 * HALF)
@@ -35,9 +37,9 @@
 
 
 def kernel(
-    x_ref, up_ref, gain_ref, wu_ref, wd_ref, grad_ref, up_out, down_out,
-    tok_n, tok_u, w, hid, dpre, g, yo_in, ya_st, nb_in, ysum, z_sum, pair_in, total, fin_st, fin_in,
-    dn, dn_sib, dn_st, dn_in, ss, rs,
+    x_hbm, up_hbm, gain_ref, wu_hbm, wd_hbm, grad_ref, up_out, down_out,
+    x_ref, tok_n, tok_u, w, hid, dpre, acc, g, yo_in, ya_st, nb_in, ysum, za_in, zb_in, pair_in, total, fin_st, fin_in,
+    dn, dn_sib, dn_st, dn_in, local, ss, rs,
 ):
     dp, tensor = lax.axis_index("dp"), lax.axis_index("tensor")
     y, zl, c = dp // 4, (dp // 2) % 2, dp % 2
@@ -55,12 +57,15 @@
     from_out, from_in = 16 + 96 * zl, 112 - 96 * zl
     mine = zl
 
+    own = pl.ds(pl.multiple_of(c * TOK, 16), TOK)
+    load_up = pltpu.make_async_copy(up_hbm, tok_u.at[own], local.at[0])
+    load_up.start()
     barrier = pltpu.get_barrier_semaphore()
     peers = [sib, xr, xl, x_far, yr, yl, z_cross, *z_same.values(), *z_other.values()]
     for peer in peers:
         pl.semaphore_signal(barrier, inc=1, device_id=peer, device_id_type=MESH)
 
-    copies, only = {}, {}
+    copies, only, summed = {}, {}, {}
 
     def make(key, src, dst, device):
         i = len(copies)
@@ -89,29 +94,45 @@
     def tok_rows(group, core, first=0, rows=TOK):
         return pl.ds(pl.multiple_of(group * GROUP + core * TOK + first, 16), rows)
 
-    gain = gain_ref[...].astype(F32).reshape(1, D)
-    own = tok_rows(0, c)
-    tok_u[own] = up_ref[...]
+    load_w = [
+        pltpu.make_async_copy(ref.at[pl.ds(pl.multiple_of(c * HALF, 16), 192)], w.at[k, pl.ds(0, 192)], local.at[1 + k])
+        for k, ref in enumerate((wu_hbm, wd_hbm))
+    ]
+    load_rest = [
+        pltpu.make_async_copy(ref.at[pl.ds(192, 16)], w.at[k, pl.ds(192, 16)], local.at[3 + k])
+        for k, ref in enumerate((wu_hbm, wd_hbm))
+    ]
+    load_x = pltpu.make_async_copy(x_hbm, x_ref, local.at[5])
+    for copy in load_w:
+        copy.start()
+
+    @pl.when(c == 0)
+    def _():
+        for copy in load_rest:
+            copy.start()
+
+    @pl.when(c == 1)
+    def _():
+        w[:, pl.ds(192, 16)] = jnp.zeros((2, 16, D), BF16)
+
+    load_x.start()
     toks = {"u": tok_u, "n": tok_n}
 
     def send_own(a):
-        send((a, "r"), toks[a].at[own], toks[a].at[tok_rows(3, c)], xr)
-        send((a, "l"), toks[a].at[own], toks[a].at[tok_rows(1, c)], xl)
-        send((a, "s0"), toks[a].at[own], toks[a].at[own], sib)
-
+        send((a, "r"), toks[a].at[own], toks[a].at[tok_rows(LEFT, c)], xr)
+        send((a, "l"), toks[a].at[own], toks[a].at[tok_rows(RIGHT, c)], xl)
+        send((a, "s", 0), toks[a].at[own], toks[a].at[own], sib)
+
+    load_up.wait()
     pl.semaphore_wait(barrier, len(peers))
     send_own("u")
-
-    for k, ref in enumerate((wu_ref, wd_ref)):
-        w[k, pl.ds(0, 192)] = ref[pl.ds(pl.multiple_of(c * HALF, 16), 192)]
-
-        @pl.when(c == 0)
-        def _():
-            w[k, pl.ds(192, 16)] = ref[pl.ds(192, 16)]
-
-        @pl.when(c == 1)
-        def _():
-            w[k, pl.ds(192, 16)] = jnp.zeros((16, D), BF16)
+    for copy in load_w:
+        copy.wait()
+
+    @pl.when(c == 0)
+    def _():
+        for copy in load_rest:
+            copy.wait()
 
     def rows_of(slot, first, rows):
         return pl.ds(pl.multiple_of(FIRST[slot] + first, 16), rows)
@@ -122,6 +143,8 @@
     for i in range(4):
         send(("w0", i), w.at[kind, chunk(0, i)], w.at[kind, chunk(1, i)], z_out)
 
+    gain = gain_ref[...].astype(F32).reshape(1, D)
+    load_x.wait()
     def norm(i, _):
         r = pl.ds(pl.multiple_of(i * 16, 16), 16)
         wide = x_ref[r].astype(F32)
@@ -133,16 +156,20 @@
     send_own("n")
 
     def pass_neighbours(a):
+        t = toks[a]
         recv((a, "r"))
-        send((a, "fr"), toks[a].at[tok_rows(3, c, 0, 64)], toks[a].at[tok_rows(2, c, 0, 64)], xr)
-        send((a, "s3"), toks[a].at[tok_rows(3, c)], toks[a].at[tok_rows(3, c)], sib)
+        send((a, "fr"), t.at[tok_rows(LEFT, c, 0, 64)], t.at[tok_rows(OPPOSITE, c, 0, 64)], xr)
+        send((a, "s", LEFT), t.at[tok_rows(LEFT, c)], t.at[tok_rows(LEFT, c)], sib)
         recv((a, "l"))
-        send((a, "fl"), toks[a].at[tok_rows(1, c, 64, 64)], toks[a].at[tok_rows(2, c, 64, 64)], xl)
-        send((a, "s1"), toks[a].at[tok_rows(1, c)], toks[a].at[tok_rows(1, c)], sib)
+        send((a, "fl"), t.at[tok_rows(RIGHT, c, 64, 64)], t.at[tok_rows(OPPOSITE, c, 64, 64)], xl)
+        send((a, "s", RIGHT), t.at[tok_rows(RIGHT, c)], t.at[tok_rows(RIGHT, c)], sib)
 
     def pass_opposite(a):
         recv((a, "fr"), (a, "fl"))
-        send((a, "s2"), toks[a].at[tok_rows(2, c)], toks[a].at[tok_rows(2, c)], sib)
+        send((a, "s", OPPOSITE), toks[a].at[tok_rows(OPPOSITE, c)], toks[a].at[tok_rows(OPPOSITE, c)], sib)
+
+    def tokens(group):
+        recv(("u", "s", group), ("n", "s", group))
 
     def share(key, rows, peer):
         send(("wy", key), w.at[kind, rows], w.at[kind, rows], peer)
@@ -150,35 +177,44 @@
     def pass_w1(i):
         recv(("w0", i))
         send(("w1", i), w.at[kind, chunk(1, i)], w.at[kind, chunk(3, i)], z_in)
-        share((1, i), chunk(1, i), (yr, yr, yl, yl)[i])
+        share((1, i), chunk(1, i), (yr, yl, yr, yl)[i])
+
+    def far_out(key, k, i):
+        if i == 0:
+            send((key, "x"), w.at[k, rows_of(3, 0, 16)], w.at[k, rows_of(2, 0, 16)], z_out, zl == 1)
+            for n in range(2):
+                here, there = rows_of(3, from_in + 48 * n, 48), rows_of(2, from_in + 48 * n, 48)
+                make((key, n), w.at[k, here], w.at[k, there], z_out)
+        pl.when(zl == 1 - i % 2)(copies[key, i // 2].start)
+
+    def far_in(key, came, k, n):
+        recv((came, n))
+        rows = rows_of(2, from_out + 48 * n, 48)
+        send((key, n), w.at[k, rows], w.at[k, rows], z_in)
+        if n == 1:
+            recv((came, "x"), when=zl == 0)
+            rows = rows_of(2, 0, 16)
+            send((key, "x"), w.at[k, rows], w.at[k, rows], z_in, zl == 0)
 
     def pass_w3(i):
         recv(("w1", i))
-        if i == 0:
-            extra = rows_of(3, 0, 16), rows_of(2, 0, 16)
-            send(("w3", "x"), w.at[kind, extra[0]], w.at[kind, extra[1]], z_out, zl == 1)
-            for n in range(2):
-                there = rows_of(2, from_in + 48 * n, 48)
-                make(("w3", n), w.at[kind, rows_of(3, from_in + 48 * n, 48)], w.at[kind, there], z_out)
-        pl.when(zl == 1 - i // 2)(copies["w3", i % 2].start)
-        share((3, i), chunk(3, i), (yl, yl, yr, yr)[i])
+        far_out("w3", kind, i)
+        share((3, i), chunk(3, i), (yl, yr, yl, yr)[i])
 
     def pass_w2(n):
-        recv(("w3", n))
-        rows = rows_of(2, from_out + 48 * n, 48)
-        send(("w2", n), w.at[kind, rows], w.at[kind, rows], z_in)
-        share((2, "o", n), rows, yr)
-        if n == 1:
-            recv(("w3", "x"), when=zl == 0)
-            rows = rows_of(2, 0, 16)
-            send(("w2", "x"), w.at[kind, rows], w.at[kind, rows], z_in, zl == 0)
-
-    def pass_last():
-        for n in range(2):
-            recv(("w2", n))
-            share((2, "i", n), rows_of(2, from_in + 48 * n, 48), yl)
-        recv(("w2", "x"), when=zl == 1)
-        share((2, "x"), rows_of(2, 0, 16), yl)
+        far_in("w2", "w3", kind, n)
+
+    def pass_v3(i):
+        recv(("wy", (3, i)))
+        far_out("v3", 1 - kind, i)
+
+    def pass_v2(n):
+        far_in("v2", "v3", 1 - kind, n)
+
+    def far_w():
+        for key in ("w2", "v2"):
+            recv((key, 0), (key, 1))
+            recv((key, "x"), when=zl == 1)
 
     def all_w(slot):
         recv(*[key for key in copies if key[0] == "wy" and key[1][0] == slot])
@@ -201,15 +237,7 @@
 
         lax.fori_loop(0, 2, one, 0)
 
-    def grads(slot, slots=1):
-        r = pl.ds(FIRST[slot], slots * HALF)
-
-        def columns(cols):
-            up = jnp.dot(dpre[r], tok_n[:, cols], preferred_element_type=F32)
-            g[0, r, cols] = (up * GRAD_SCALE).astype(BF16)
-            down = jnp.dot(hid[r], tok_u[:, cols], preferred_element_type=F32)
-            g[1, r, cols] = (down * GRAD_SCALE).astype(BF16)
-
+    def all_columns(columns):
         def tile(n, _):
             columns(pl.ds(pl.multiple_of(n * 512, 512), 512))
             return 0
@@ -217,6 +245,35 @@
         lax.fori_loop(0, 3, tile, 0)
         columns(pl.ds(1536, 128))
 
+    def grads(kind, slot, slots=1):
+        r = pl.ds(FIRST[slot], slots * HALF)
+        left, right = ((dpre, tok_n), (hid, tok_u))[kind]
+
+        def columns(cols):
+            term = jnp.dot(left[r], right[:, cols], preferred_element_type=F32)
+            g[kind, r, cols] = (term * GRAD_SCALE).astype(BF16)
+
+        all_columns(columns)
+
+    def grads_first(kind):
+        r, t = pl.ds(0, HALF), pl.ds(0, 3 * GROUP)
+        left, right = ((dpre, tok_n), (hid, tok_u))[kind]
+
+        def columns(cols):
+            acc[kind, :, cols] = jnp.dot(left[r, t], right[t, cols], preferred_element_type=F32)
+
+        all_columns(columns)
+
+    def grads_last(kind):
+        r, t = pl.ds(0, HALF), pl.ds(3 * GROUP, GROUP)
+        left, right = ((dpre, tok_n), (hid, tok_u))[kind]
+
+        def columns(cols):
+            term = acc[kind, :, cols] + jnp.dot(left[r, t], right[t, cols], preferred_element_type=F32)
+            g[kind, r, cols] = (term * GRAD_SCALE).astype(BF16)
+
+        all_columns(columns)
+
     def window(owner, first=0, cols=WIN):
         return pl.ds(pl.multiple_of(((owner + 8) % 4) * 384 + first, 128), cols)
 
@@ -227,7 +284,7 @@
         return pl.ds(pl.multiple_of(FIRST[slot] + i * 16, 16), 16)
 
     def kinds(part):
-        return pl.ds(0, 2) if part[1] is None else pl.ds(part[1], 1)
+        return pl.ds(0, 2) if part[1] is None else pl.ds(mine if part[1] == "mine" else part[1], 1)
 
     def y1(*part):
         r, k = pl.ds(FIRST[part[0]], HALF), kinds(part)
@@ -268,29 +325,53 @@
             return 0
 
         lax.fori_loop(0, HALF // 16, add, 0)
-        if slot == 2:
-            send(("zb", 2), ysum.at[2, 1 - mine], z_sum.at[1], z_other[2])
-            send(("za", 2), ysum.at[2, mine], z_sum.at[2], z_same[2])
-        elif slot == 0:
-            if ("zb", 0) not in copies:
-                make(("zb", 0), ysum.at[0, 1 - mine], z_sum.at[0], z_other[0])
-            pl.when(mine != part[1])(copies["zb", 0].start)
-        else:
-            send(("zb", slot), ysum.at[slot, part[1]], z_sum.at[3], z_other[slot], mine != part[1])
-            send(("za", slot), ysum.at[slot, part[1]], z_sum.at[4], z_same[slot], mine == part[1])
-
-    def pair_send(k):
-        send(("pair", k), g.at[k, pl.ds(FIRST[(3, 1)[k]], HALF)], pair_in.at[k], (z_in, z_out)[k])
-
-    def pair_add(k):
-        recv(("pair", k))
+        summed.setdefault(slot, []).append(part[1])
+        if part[1] == "mine":
+            send(("za", slot), ysum.at[slot, mine], za_in.at[slot - 1], z_same[slot])
+            return
+        if ("zb", slot) not in copies:
+            make(("zb", slot), ysum.at[slot, 1 - mine], zb_in.at[slot], z_other[slot])
+            if slot:
+                make(("za", slot), ysum.at[slot, mine], za_in.at[slot - 1], z_same[slot])
+        for key, when in (("zb", mine != part[1]), ("za", mine == part[1])):
+            if (key, slot) in copies:
+                if part[1] is None:
+                    copies[key, slot].start()
+                else:
+                    pl.when(when)(copies[key, slot].start)
+
+    def presum_send(key, kind, slot, device):
+        send(key, g.at[kind, pl.ds(FIRST[slot], HALF)], pair_in.at[PRE.index(key)], device)
+
+    def presum_add(key, kind, slot):
+        recv(key)
 
         def add(i, _):
-            here = slot16((1, 0)[k], i)
-            g[k, here] = (g[k, here].astype(F32) + pair_in[k, rows16(i)].astype(F32)).astype(BF16)
+            here = slot16(slot, i)
+            g[kind, here] = (
+                g[kind, here].astype(F32) + pair_in[PRE.index(key), rows16(i)].astype(F32)
+            ).astype(BF16)
             return 0
 
         lax.fori_loop(0, HALF // 16, add, 0)
+
+    def outer_send():
+        presum_send("outer", 1, 1, z_out)
+
+    def outer_add():
+        presum_add("outer", 1, 0)
+
+    def inner_send():
+        presum_send("inner", 0, 3, z_in)
+
+    def inner_add():
+        presum_add("inner", 0, 1)
+
+    def swap_send():
+        presum_send("swap", 1 - mine, 2, z_in)
+
+    def swap_add():
+        presum_add("swap", mine, 2)
 
     def back(group):
         t = pl.ds(group * GROUP, GROUP)
@@ -301,12 +382,7 @@
             dn[group, 0, :, cols] = part[:TOK]
             dn[group, 1, :, cols] = part[TOK:]
 
-        def tile(n, _):
-            columns(pl.ds(pl.multiple_of(n * 512, 512), 512))
-            return 0
-
-        lax.fori_loop(0, 3, tile, 0)
-        columns(pl.ds(1536, 128))
+        all_columns(columns)
         send(("dn", group), dn.at[group, 1 - c], dn_sib.at[group], sib)
 
     def dn_pass(group, peer):
@@ -323,57 +399,70 @@
     pass_w1(0)
     pass_neighbours("u")
     pass_w1(1)
-    recv(("u", "s0"), ("n", "s0"))
+    tokens(0)
     forward_one(0, 0)
     pass_w1(2)
     pass_w3(0)
     pass_w1(3)
-    pass_neighbours("n")
     pass_w3(1)
     pass_w3(2)
-    recv(("u", "s1"), ("n", "s1"))
-    forward_one(0, 1)
+    pass_neighbours("n")
     pass_w3(3)
+    pass_v3(0)
+    pass_w2(0)
+    tokens(RIGHT)
+    forward_one(0, RIGHT)
+    pass_v3(1)
+    tokens(LEFT)
+    forward_one(0, LEFT)
     pass_opposite("u")
-    recv(("u", "s3"), ("n", "s3"))
-    forward_one(0, 3)
-    pass_w2(0)
+    pass_v3(2)
+    pass_w2(1)
+    grads_first(0)
+    grads_first(1)
+    pass_v3(3)
+    pass_v2(0)
     pass_opposite("n")
-    recv(("u", "s2"), ("n", "s2"))
-    forward_one(0, 2)
-    pass_w2(1)
-    grads(0)
+    all_w(1)
+    forward_one(1, 0)
+    forward_one(1, RIGHT)
+    tokens(OPPOSITE)
+    forward_one(0, OPPOSITE)
+    grads_last(0)
     y1(0, 0)
-    pass_last()
-    all_w(1)
-    all_w(3)
-    forward_all(1, 2)
+    pass_v2(1)
+    forward_one(1, LEFT)
+    forward_one(1, OPPOSITE)
+    forward_all(3)
     y2(0, 0)
+    grads(1, 1, 2)
+    y1(3, 1)
+    outer_send()
+    grads(0, 1, 2)
+    inner_send()
+    far_w()
+    forward_all(2)
+    y3(0, 0)
+    grads(0, 2)
+    y2(3, 1)
     grads(1, 2)
-    pair_send(1)
-    pair_send(0)
-    y1(3, 1)
-    all_w(2)
-    forward_all(2)
-    grads(2)
     y1(2, None)
-    y2(3, 1)
-    y3(0, 0)
-    back(2)
-    back(1)
-    dn_pass(2, x_far)
+    grads_last(1)
+    back(OPPOSITE)
+    back(RIGHT)
+    dn_pass(OPPOSITE, x_far)
     y2(2, None)
-    pair_add(1)
+    back(LEFT)
+    dn_pass(RIGHT, xr)
+    y3(3, 1)
+    outer_add()
     y1(0, 1)
-    back(3)
-    dn_pass(1, xr)
-    pair_add(0)
+    inner_add()
     y1(1, 0)
     back(0)
-    y3(3, 1)
-    dn_pass(3, xl)
+    y3(2, None)
+    dn_pass(LEFT, xl)
     y2(0, 1)
-    y3(2, None)
     y2(1, 0)
     y3(0, 1)
     y3(1, 0)
@@ -390,25 +479,37 @@
             dnormed += dn_in[k, here].astype(F32)
         dunit = dnormed * gain
         project = jnp.mean(dunit * unit, axis=-1, keepdims=True)
-        grad_ref[here] = (up_ref[here].astype(F32) + inv * (dunit - unit * project)).astype(BF16)
+        grad_ref[here] = (tok_u[tok_rows(0, c, i * 16, 16)].astype(F32) + inv * (dunit - unit * project)).astype(BF16)
         return 0
 
     lax.fori_loop(0, TOK // 16, finish, 0)
 
-    recv(("zb", 0), ("zb", 2), ("za", 2))
-    recv(("zb", 1), ("za", 1), when=mine == 0)
-    recv(("zb", 3), ("za", 3), when=mine == 1)
+    pieces = []
+    for slot, parts in summed.items():
+        for key, ref in (("za", za_in.at[slot - 1]), ("zb", zb_in.at[slot])):
+            if (key, slot) not in copies:
+                continue
+            pieces.append(ref)
+            if slot and parts in ([0], [1]):
+                only[key, slot] = (mine == parts[0]) if key == "za" else (mine != parts[0])
+                recv((key, slot), when=mine == parts[0])
+
+                @pl.when(mine != parts[0])
+                def _():
+                    ref[...] = jnp.zeros((HALF, WIN), BF16)
+            else:
+                recv((key, slot))
     total[:, pl.ds(WIN, 128)] = jnp.zeros((16, 128), F32)
 
     def split(i, _):
         here = rows16(i)
         rows = ysum[0, mine, here].astype(F32)
-        for k in range(5):
-            rows += z_sum[k, here].astype(F32)
+        for piece in pieces:
+            rows += piece[here].astype(F32)
         total[:, pl.ds(0, WIN)] = rows
+        turned = pltpu.roll(total[...], WIN + 128 - 32 * y, 1)
         for q in range(4):
-            turned = pltpu.roll(total[...], (WIN + 128 - 104 * q) - 32 * y, 1)
-            fin_st[q, here] = turned[:, :128].astype(BF16)
+            fin_st[q, here] = turned[:, 104 * q : 104 * q + 128].astype(BF16)
         return 0
 
     lax.fori_loop(0, HALF // 16, split, 0)
@@ -436,6 +537,7 @@
 
 def body(inputs, gain, w_up, w_down, upstream):
     vmem = pl.BlockSpec(memory_space=pltpu.VMEM)
+    hbm = pl.BlockSpec(memory_space=pl.ANY)
     input_grad, up_grad, down_grad = pl.pallas_call(
         kernel,
         out_shape=(
@@ -443,21 +545,24 @@
             jax.ShapeDtypeStruct((400, 104), F32),
             jax.ShapeDtypeStruct((400, 104), F32),
         ),
-        in_specs=[vmem] * 5,
+        in_specs=[hbm, hbm, vmem, hbm, hbm],
         out_specs=(vmem,) * 3,
         scratch_shapes=[
+            pltpu.VMEM((TOK, D), BF16),
             pltpu.VMEM((T, D), BF16),
             pltpu.VMEM((T, D), BF16),
             pltpu.VMEM((2, HID, D), BF16),
             pltpu.VMEM((HID, T), BF16),
             pltpu.VMEM((HID, T), BF16),
+            pltpu.VMEM((2, HALF, D), F32),
             pltpu.VMEM((2, HID, D), BF16),
             pltpu.VMEM((4, 2, 2, HALF, 256), BF16),
             pltpu.VMEM((4, 2, 2, HALF, 256), BF16),
             pltpu.VMEM((4, 2, 2, HALF, WIN), BF16),
             pltpu.VMEM((4, 2, HALF, WIN), BF16),
-            pltpu.VMEM((5, HALF, WIN), BF16),
-            pltpu.VMEM((2, HALF, D), BF16),
+            pltpu.VMEM((3, HALF, WIN), BF16),
+            pltpu.VMEM((4, HALF, WIN), BF16),
+            pltpu.VMEM((3, HALF, D), BF16),
             pltpu.VMEM((16, WIN + 128), F32),
             pltpu.VMEM((4, HALF, 128), BF16),
             pltpu.VMEM((4, HALF, 128), BF16),
@@ -465,6 +570,7 @@
             pltpu.VMEM((4, TOK, D), BF16),
             pltpu.VMEM((3, TOK, D), BF16),
             pltpu.VMEM((3, TOK, D), BF16),
+            pltpu.SemaphoreType.DMA((6,)),
             pltpu.SemaphoreType.DMA((N_SEM,)),
             pltpu.SemaphoreType.DMA((N_SEM,)),
         ],

time: 123 us -> 117 us (0.951)
  Pallas kernels: 118 us -> 112 us
    pallas_call x1, Pallas kernels: 118 us -> 112 us  [body(): pl.pallas_call(kernel, out_shape=(jax.ShapeDtypeStruct((TOK, D), BF16), j...]
where the time goes in v6:
time: 117 us; the launch traced here: 116 us
  Pallas kernels  112 us (96%)
  local copies, waits for them, and re-layouts  4.14 us (4%)
    pallas_call x1, Pallas kernels, body(): pl.pallas_call(kernel, out_shape=(jax.ShapeDtypeStruct((TOK, D), BF16), j...  112 us
    unnamed x5, local copies, waits for them, and re-layouts  4.14 us

profile of v6, /device:TPU:1, one launch (start us, length us, event | category | flops | bytes accessed | tf_op | source)
XLA Modules:
  0.0 116.5 jit_solution(8482340446850661345)
XLA Ops:
  0.6 111.7 %block_backward.1 = (bf16[128,1664]{1,0:T(8,128)(2,1)}, f32[400,104]{1,0:T(8,128)}, f32[400,104]{1,0:T(8,128)}) custom-call(bf16[128,1664]{1,0:T(8,128)(2,1)} %x_hbm.1, bf16[128,1664]{1,0:T(8,128)(2,1)} %up_hbm.1, bf16[1664]{0:T(1024)(128)(2,1)} %gain_ref.1, bf16[400,1664]{1,0:T(8,128)(2,1)} %bitcast.2, bf16[400,1664]{1,0:T(8,128)(2,1)} %wd_hbm.1), custom_call_target="tpu_custom_call" | custom-call | tf_op jit(solution)/shard_map/block_backward/pallas_call | solution.py:541
  112.3 0.0 copy-start
  112.3 1.8 %copy.11 = bf16[128,1664]{1,0:T(8,128)(2,1)} copy(bf16[128,1664]{1,0:T(8,128)(2,1)} %get-tuple-element.12) | data formatting | bytes 851968
  114.2 1.6 %copy.12 = f32[104,400]{0,1:T(8,128)} copy(f32[104,400]{0,1:T(8,128)} %bitcast.3) | data formatting | bytes 332800
  115.8 0.0 copy-done
  115.8 0.7 copy.13
Async XLA Ops:
  112.3 3.5 %copy-start = (f32[400,104]{1,0:T(8,128)S(1)}, f32[400,104]{1,0:T(8,128)}, u32[]{:S(2)}) copy-start(f32[400,104]{1,0:T(8,128)} %get-tuple-element.14) | copy-start | bytes 499204

commit v7 on v6

--- a/solution.py
+++ b/solution.py
@@ -6,7 +6,7 @@
 from jax.sharding import PartitionSpec as P
 
 MESH = pl.DeviceIdType.MESH
-PRE = ("outer", "inner", "swap")
+PRE = ("outer", "inner")
 F32, BF16 = jnp.float32, jnp.bfloat16
 
 norm_eps = 1e-06
@@ -18,7 +18,7 @@
 HID = 4 * HALF
 WIN = 512
 CHUNKS = ((0, 64), (112, 48), (64, 48), (160, 48))
-N_SEM = 96
+N_SEM = 104
 RIGHT, LEFT, OPPOSITE = 1, 2, 3
 GRAD_SCALE = float(32768) ** (-0.5)
 
@@ -260,7 +260,7 @@
         left, right = ((dpre, tok_n), (hid, tok_u))[kind]
 
         def columns(cols):
-            acc[kind, :, cols] = jnp.dot(left[r, t], right[t, cols], preferred_element_type=F32)
+            acc[:, cols] = jnp.dot(left[r, t], right[t, cols], preferred_element_type=F32)
 
         all_columns(columns)
 
@@ -269,7 +269,7 @@
         left, right = ((dpre, tok_n), (hid, tok_u))[kind]
 
         def columns(cols):
-            term = acc[kind, :, cols] + jnp.dot(left[r, t], right[t, cols], preferred_element_type=F32)
+            term = acc[:, cols] + jnp.dot(left[r, t], right[t, cols], preferred_element_type=F32)
             g[kind, r, cols] = (term * GRAD_SCALE).astype(BF16)
 
         all_columns(columns)
@@ -288,9 +288,12 @@
 
     def y1(*part):
         r, k = pl.ds(FIRST[part[0]], HALF), kinds(part)
-        left, right = pl.ds(0, 256), pl.ds(256, 256)
         send(("yo", part, 0), g.at[k, r, window(y + 2, 0, 256)], yo_in.at[part[0], 0, k], yr)
         send(("yo", part, 1), g.at[k, r, window(y + 2, 256, 256)], yo_in.at[part[0], 1, k], yl)
+
+    def yd(*part):
+        r, k = pl.ds(FIRST[part[0]], HALF), kinds(part)
+        left, right = pl.ds(0, 256), pl.ds(256, 256)
         send(("yd", part, 0), g.at[k, r, window(y + 1, 256, 256)], nb_in.at[part[0], 0, k, :, right], yr)
         send(("yd", part, 1), g.at[k, r, window(y - 1, 0, 256)], nb_in.at[part[0], 1, k, :, left], yl)
 
@@ -367,12 +370,6 @@
     def inner_add():
         presum_add("inner", 0, 1)
 
-    def swap_send():
-        presum_send("swap", 1 - mine, 2, z_in)
-
-    def swap_add():
-        presum_add("swap", mine, 2)
-
     def back(group):
         t = pl.ds(group * GROUP, GROUP)
         rows = dpre[:, t].T
@@ -395,6 +392,24 @@
 
         lax.fori_loop(0, TOK // 16, add, 0)
         send(("dx", group), dn_st.at[group - 1], dn_in.at[group - 1], peer)
+
+    def input_gradient():
+        recv(("dn", 0), ("dx", 1), ("dx", 2), ("dx", 3))
+
+        def finish(i, _):
+            here = rows16(i)
+            wide = x_ref[here].astype(F32)
+            inv = lax.rsqrt(jnp.mean(wide * wide, axis=-1, keepdims=True) + norm_eps)
+            unit = wide * inv
+            dnormed = dn[0, c, here].astype(F32) + dn_sib[0, here].astype(F32)
+            for k in range(3):
+                dnormed += dn_in[k, here].astype(F32)
+            dunit = dnormed * gain
+            project = jnp.mean(dunit * unit, axis=-1, keepdims=True)
+            grad_ref[here] = (tok_u[tok_rows(0, c, i * 16, 16)].astype(F32) + inv * (dunit - unit * project)).astype(BF16)
+            return 0
+
+        lax.fori_loop(0, TOK // 16, finish, 0)
 
     pass_w1(0)
     pass_neighbours("u")
@@ -419,70 +434,58 @@
     pass_v3(2)
     pass_w2(1)
     grads_first(0)
-    grads_first(1)
+    pass_opposite("n")
     pass_v3(3)
-    pass_v2(0)
-    pass_opposite("n")
-    all_w(1)
-    forward_one(1, 0)
-    forward_one(1, RIGHT)
     tokens(OPPOSITE)
     forward_one(0, OPPOSITE)
     grads_last(0)
     y1(0, 0)
+    yd(0, 0)
+    pass_v2(0)
+    all_w(1)
+    forward_all(1, 2)
     pass_v2(1)
-    forward_one(1, LEFT)
-    forward_one(1, OPPOSITE)
-    forward_all(3)
     y2(0, 0)
     grads(1, 1, 2)
     y1(3, 1)
+    yd(3, 1)
     outer_send()
     grads(0, 1, 2)
     inner_send()
     far_w()
     forward_all(2)
+    y2(3, 1)
+    grads(0, 2)
+    y1(2, 0)
+    grads(1, 2)
+    y1(2, 1)
+    yd(2, 0)
     y3(0, 0)
-    grads(0, 2)
-    y2(3, 1)
-    grads(1, 2)
-    y1(2, None)
-    grads_last(1)
+    grads(1, 0)
     back(OPPOSITE)
+    y2(2, 0)
+    yd(2, 1)
     back(RIGHT)
     dn_pass(OPPOSITE, x_far)
-    y2(2, None)
-    back(LEFT)
+    y2(2, 1)
+    outer_add()
+    y1(0, 1)
     dn_pass(RIGHT, xr)
     y3(3, 1)
-    outer_add()
-    y1(0, 1)
+    back(LEFT)
+    y3(2, 0)
     inner_add()
     y1(1, 0)
+    yd(0, 1)
+    dn_pass(LEFT, xl)
     back(0)
-    y3(2, None)
-    dn_pass(LEFT, xl)
+    y3(2, 1)
     y2(0, 1)
+    yd(1, 0)
     y2(1, 0)
     y3(0, 1)
     y3(1, 0)
-
-    recv(("dn", 0), ("dx", 1), ("dx", 2), ("dx", 3))
-
-    def finish(i, _):
-        here = rows16(i)
-        wide = x_ref[here].astype(F32)
-        inv = lax.rsqrt(jnp.mean(wide * wide, axis=-1, keepdims=True) + norm_eps)
-        unit = wide * inv
-        dnormed = dn[0, c, here].astype(F32) + dn_sib[0, here].astype(F32)
-        for k in range(3):
-            dnormed += dn_in[k, here].astype(F32)
-        dunit = dnormed * gain
-        project = jnp.mean(dunit * unit, axis=-1, keepdims=True)
-        grad_ref[here] = (tok_u[tok_rows(0, c, i * 16, 16)].astype(F32) + inv * (dunit - unit * project)).astype(BF16)
-        return 0
-
-    lax.fori_loop(0, TOK // 16, finish, 0)
+    input_gradient()
 
     pieces = []
     for slot, parts in summed.items():
@@ -554,7 +557,7 @@
             pltpu.VMEM((2, HID, D), BF16),
             pltpu.VMEM((HID, T), BF16),
             pltpu.VMEM((HID, T), BF16),
-            pltpu.VMEM((2, HALF, D), F32),
+            pltpu.VMEM((HALF, D), F32),
             pltpu.VMEM((2, HID, D), BF16),
             pltpu.VMEM((4, 2, 2, HALF, 256), BF16),
             pltpu.VMEM((4, 2, 2, HALF, 256), BF16),
@@ -562,7 +565,7 @@
             pltpu.VMEM((4, 2, HALF, WIN), BF16),
             pltpu.VMEM((3, HALF, WIN), BF16),
             pltpu.VMEM((4, HALF, WIN), BF16),
-            pltpu.VMEM((3, HALF, D), BF16),
+            pltpu.VMEM((2, HALF, D), BF16),
             pltpu.VMEM((16, WIN + 128), F32),
             pltpu.VMEM((4, HALF, 128), BF16),
             pltpu.VMEM((4, HALF, 128), BF16),
@@ -575,7 +578,7 @@
             pltpu.SemaphoreType.DMA((N_SEM,)),
         ],
         compiler_params=pltpu.CompilerParams(
-            collective_id=1, has_side_effects=True, vmem_limit_bytes=60 * 2**20
+            collective_id=1, has_side_effects=True, vmem_limit_bytes=53 * 2**20
         ),
         name="block_backward",
     )(inputs, upstream, gain, w_up.T, w_down)

time: 117 us -> 111 us (0.949)
  Pallas kernels: 112 us -> 108 us
  local copies, waits for them, and re-layouts: 4.14 us -> 2.8 us
    pallas_call x1, Pallas kernels: 112 us -> 108 us  [body(): pl.pallas_call(kernel, out_shape=(jax.ShapeDtypeStruct((TOK, D), BF16), j...]
    unnamed x5, local copies, waits for them, and re-layouts: 4.14 us -> 2.8 us
where the time goes in v7:
time: 111 us
  Pallas kernels  108 us (97%)
  local copies, waits for them, and re-layouts  2.8 us (3%)
    pallas_call x1, Pallas kernels, body(): pl.pallas_call(kernel, out_shape=(jax.ShapeDtypeStruct((TOK, D), BF16), j...  108 us
    unnamed x5, local copies, waits for them, and re-layouts  2.8 us

profile of v7, /device:TPU:1, one launch (start us, length us, event | category | flops | bytes accessed | tf_op | source)
XLA Modules:
  0.0 111.0 jit_solution(9928969190368216759)
XLA Ops:
  0.6 0.0 copy-start
  0.6 0.7 copy-done
  1.3 107.5 %block_backward.1 = (bf16[128,1664]{1,0:T(8,128)(2,1)S(1)}, f32[400,104]{1,0:T(8,128)S(1)}, f32[400,104]{1,0:T(8,128)S(1)}) custom-call(bf16[128,1664]{1,0:T(8,128)(2,1)} %x_hbm.1, bf16[128,1664]{1,0:T(8,128)(2,1)} %up_hbm.1, bf16[1664]{0:T(1024)(128)(2,1)S(1)} %copy-done, bf16[400,1664]{1,0:T(8,128)(2,1)} %bitcast.3, bf16[400,1664]{1,0:T(8,128)(2,1)} %wd_hbm.1), custom_call_target="tpu_custom_call" | custom-call | tf_op jit(solution)/shard_map/block_backward/pallas_call | solution.py:544
  108.9 0.8 copy.11
  109.6 0.7 copy.12
  110.3 0.7 copy.13
Async XLA Ops:
  0.6 0.7 copy-start

commit v8 on v7

--- a/solution.py
+++ b/solution.py
@@ -18,7 +18,7 @@
 HID = 4 * HALF
 WIN = 512
 CHUNKS = ((0, 64), (112, 48), (64, 48), (160, 48))
-N_SEM = 104
+N_SEM = 112
 RIGHT, LEFT, OPPOSITE = 1, 2, 3
 GRAD_SCALE = float(32768) ** (-0.5)
 
@@ -462,33 +462,33 @@
     yd(2, 0)
     y3(0, 0)
     grads(1, 0)
+    y3(3, 1)
     back(OPPOSITE)
     y2(2, 0)
     yd(2, 1)
     back(RIGHT)
     dn_pass(OPPOSITE, x_far)
     y2(2, 1)
+    dn_pass(RIGHT, xr)
+    inner_add()
+    y1(1, 0)
+    y3(2, 0)
     outer_add()
     y1(0, 1)
-    dn_pass(RIGHT, xr)
-    y3(3, 1)
     back(LEFT)
-    y3(2, 0)
-    inner_add()
-    y1(1, 0)
+    y3(2, 1)
+    yd(1, 0)
+    dn_pass(LEFT, xl)
+    y2(1, 0)
+    back(0)
     yd(0, 1)
-    dn_pass(LEFT, xl)
-    back(0)
-    y3(2, 1)
     y2(0, 1)
-    yd(1, 0)
-    y2(1, 0)
+    y3(1, 0)
     y3(0, 1)
-    y3(1, 0)
     input_gradient()
 
-    pieces = []
-    for slot, parts in summed.items():
+    def arrived(slot):
+        pieces, parts = [], summed[slot]
         for key, ref in (("za", za_in.at[slot - 1]), ("zb", zb_in.at[slot])):
             if (key, slot) not in copies:
                 continue
@@ -502,12 +502,26 @@
                     ref[...] = jnp.zeros((HALF, WIN), BF16)
             else:
                 recv((key, slot))
+        return pieces
+
     total[:, pl.ds(WIN, 128)] = jnp.zeros((16, 128), F32)
+    early = arrived(3) + arrived(2)
+
+    def add_early(i, _):
+        here = rows16(i)
+        rows = ysum[0, mine, here].astype(F32)
+        for piece in early:
+            rows += piece[here].astype(F32)
+        acc[here, pl.ds(0, WIN)] = rows
+        return 0
+
+    lax.fori_loop(0, HALF // 16, add_early, 0)
+    late = arrived(0) + arrived(1)
 
     def split(i, _):
         here = rows16(i)
-        rows = ysum[0, mine, here].astype(F32)
-        for piece in pieces:
+        rows = acc[here, pl.ds(0, WIN)]
+        for piece in late:
             rows += piece[here].astype(F32)
         total[:, pl.ds(0, WIN)] = rows
         turned = pltpu.roll(total[...], WIN + 128 - 32 * y, 1)
@@ -515,17 +529,20 @@
             fin_st[q, here] = turned[:, 104 * q : 104 * q + 128].astype(BF16)
         return 0
 
-    lax.fori_loop(0, HALF // 16, split, 0)
     me = 2 * zl + c
-    for key, device, to in (("sib", sib, 2 * zl + 1 - c), ("in", z_in, 2 * (1 - zl) + c), ("cross", z_cross, 2 * (1 - zl) + 1 - c)):
-        send(("f", key), fin_st.at[to], fin_in.at[me], device)
+    others = (("in", z_in, 2 * (1 - zl) + c), ("cross", z_cross, 2 * (1 - zl) + 1 - c), ("sib", sib, 2 * zl + 1 - c))
+    for n, (first, rows) in enumerate(((0, 112), (112, 96))):
+        lax.fori_loop(first // 16, (first + rows) // 16, split, 0)
+        part = pl.ds(first, rows)
+        for key, device, to in others:
+            send(("f", key, n), fin_st.at[to, part], fin_in.at[me, part], device)
 
     def keep(i, _):
         fin_in[me, rows16(i)] = fin_st[me, rows16(i)]
         return 0
 
     lax.fori_loop(0, HALF // 16, keep, 0)
-    recv(("f", "sib"), ("f", "in"), ("f", "cross"))
+    recv(*[("f", key, n) for n in range(2) for key in ("sib", "in", "cross")])
 
     for q in range(2):
         rows = (HALF, 400 - HALF)[q]

time: 111 us -> 110 us (level)
  no operation moved by 1% of the time
where the time goes in v8:
time: 110 us
  Pallas kernels  107 us (97%)
  local copies, waits for them, and re-layouts  2.8 us (3%)
    pallas_call x1, Pallas kernels, body(): pl.pallas_call(kernel, out_shape=(jax.ShapeDtypeStruct((TOK, D), BF16), j...  107 us
    unnamed x5, local copies, waits for them, and re-layouts  2.8 us

profile of v8, /device:TPU:1, one launch (start us, length us, event | category | flops | bytes accessed | tf_op | source)
XLA Modules:
  0.0 110.2 jit_solution(16510455668646739903)
XLA Ops:
  0.6 0.0 copy-start
  0.6 0.7 copy-done
  1.3 106.7 %block_backward.1 = (bf16[128,1664]{1,0:T(8,128)(2,1)S(1)}, f32[400,104]{1,0:T(8,128)S(1)}, f32[400,104]{1,0:T(8,128)S(1)}) custom-call(bf16[128,1664]{1,0:T(8,128)(2,1)} %x_hbm.1, bf16[128,1664]{1,0:T(8,128)(2,1)} %up_hbm.1, bf16[1664]{0:T(1024)(128)(2,1)S(1)} %copy-done, bf16[400,1664]{1,0:T(8,128)(2,1)} %bitcast.3, bf16[400,1664]{1,0:T(8,128)(2,1)} %wd_hbm.1), custom_call_target="tpu_custom_call" | custom-call | tf_op jit(solution)/shard_map/block_backward/pallas_call | solution.py:561
  108.1 0.8 copy.11
  108.8 0.7 copy.12
  109.5 0.7 copy.13
Async XLA Ops:
  0.6 0.7 copy-start

commit v9 on v8

--- a/solution.py
+++ b/solution.py
@@ -152,7 +152,7 @@
         tok_n[tok_rows(0, c, i * 16, 16)] = (wide * inv * gain).astype(BF16)
         return 0
 
-    lax.fori_loop(0, TOK // 16, norm, 0)
+    lax.fori_loop(0, TOK // 16, norm, 0, unroll=True)
     send_own("n")
 
     def pass_neighbours(a):
@@ -310,7 +310,7 @@
                 ).astype(BF16)
                 return 0
 
-            lax.fori_loop(0, HALF // 16, add, 0)
+            lax.fori_loop(0, HALF // 16, add, 0, unroll=True)
             send(("ya", part, way), ya_st.at[slot, way, k], nb_in.at[slot, way, k, :, pl.ds(first, 256)], peer)
 
     def y3(*part):
@@ -327,7 +327,7 @@
             ).astype(BF16)
             return 0
 
-        lax.fori_loop(0, HALF // 16, add, 0)
+        lax.fori_loop(0, HALF // 16, add, 0, unroll=True)
         summed.setdefault(slot, []).append(part[1])
         if part[1] == "mine":
             send(("za", slot), ysum.at[slot, mine], za_in.at[slot - 1], z_same[slot])
@@ -356,7 +356,7 @@
             ).astype(BF16)
             return 0
 
-        lax.fori_loop(0, HALF // 16, add, 0)
+        lax.fori_loop(0, HALF // 16, add, 0, unroll=True)
 
     def outer_send():
         presum_send("outer", 1, 1, z_out)
@@ -390,7 +390,7 @@
             dn_st[group - 1, here] = (dn[group, c, here].astype(F32) + dn_sib[group, here].astype(F32)).astype(BF16)
             return 0
 
-        lax.fori_loop(0, TOK // 16, add, 0)
+        lax.fori_loop(0, TOK // 16, add, 0, unroll=True)
         send(("dx", group), dn_st.at[group - 1], dn_in.at[group - 1], peer)
 
     def input_gradient():
@@ -469,22 +469,22 @@
     back(RIGHT)
     dn_pass(OPPOSITE, x_far)
     y2(2, 1)
+    outer_add()
+    y1(0, 1)
     dn_pass(RIGHT, xr)
+    y3(2, 0)
     inner_add()
     y1(1, 0)
-    y3(2, 0)
-    outer_add()
-    y1(0, 1)
     back(LEFT)
     y3(2, 1)
+    yd(0, 1)
+    dn_pass(LEFT, xl)
+    y2(0, 1)
+    back(0)
     yd(1, 0)
-    dn_pass(LEFT, xl)
     y2(1, 0)
-    back(0)
-    yd(0, 1)
-    y2(0, 1)
+    y3(0, 1)
     y3(1, 0)
-    y3(0, 1)
     input_gradient()
 
     def arrived(slot):
@@ -515,7 +515,7 @@
         acc[here, pl.ds(0, WIN)] = rows
         return 0
 
-    lax.fori_loop(0, HALF // 16, add_early, 0)
+    lax.fori_loop(0, HALF // 16, add_early, 0, unroll=True)
     late = arrived(0) + arrived(1)
 
     def split(i, _):
@@ -532,7 +532,7 @@
     me = 2 * zl + c
     others = (("in", z_in, 2 * (1 - zl) + c), ("cross", z_cross, 2 * (1 - zl) + 1 - c), ("sib", sib, 2 * zl + 1 - c))
     for n, (first, rows) in enumerate(((0, 112), (112, 96))):
-        lax.fori_loop(first // 16, (first + rows) // 16, split, 0)
+        lax.fori_loop(first // 16, (first + rows) // 16, split, 0, unroll=True)
         part = pl.ds(first, rows)
         for key, device, to in others:
             send(("f", key, n), fin_st.at[to, part], fin_in.at[me, part], device)

time: 110 us -> 109 us (level)
  no operation moved by 1% of the time
where the time goes in v9:
time: 109 us
  Pallas kernels  106 us (97%)
  local copies, waits for them, and re-layouts  2.8 us (3%)
    pallas_call x1, Pallas kernels, body(): pl.pallas_call(kernel, out_shape=(jax.ShapeDtypeStruct((TOK, D), BF16), j...  106 us
    unnamed x5, local copies, waits for them, and re-layouts  2.8 us

profile of v9, /device:TPU:1, one launch (start us, length us, event | category | flops | bytes accessed | tf_op | source)
XLA Modules:
  0.0 109.2 jit_solution(504874293965160858)
XLA Ops:
  0.6 0.0 copy-start
  0.6 0.7 copy-done
  1.3 105.8 %block_backward.1 = (bf16[128,1664]{1,0:T(8,128)(2,1)S(1)}, f32[400,104]{1,0:T(8,128)S(1)}, f32[400,104]{1,0:T(8,128)S(1)}) custom-call(bf16[128,1664]{1,0:T(8,128)(2,1)} %x_hbm.1, bf16[128,1664]{1,0:T(8,128)(2,1)} %up_hbm.1, bf16[1664]{0:T(1024)(128)(2,1)S(1)} %copy-done, bf16[400,1664]{1,0:T(8,128)(2,1)} %bitcast.3, bf16[400,1664]{1,0:T(8,128)(2,1)} %wd_hbm.1), custom_call_target="tpu_custom_call" | custom-call | tf_op jit(solution)/shard_map/block_backward/pallas_call | solution.py:561
  107.1 0.8 copy.11
  107.9 0.7 copy.12
  108.5 0.7 copy.13
Async XLA Ops:
  0.6 0.7 copy-start

commit v10 on v9

--- a/solution.py
+++ b/solution.py
@@ -235,14 +235,14 @@
             forward(pl.ds(FIRST[slot], slots * HALF), pl.ds(pl.multiple_of(i * 512, 512), 512))
             return 0
 
-        lax.fori_loop(0, 2, one, 0)
+        lax.fori_loop(0, 2, one, 0, unroll=True)
 
     def all_columns(columns):
         def tile(n, _):
             columns(pl.ds(pl.multiple_of(n * 512, 512), 512))
             return 0
 
-        lax.fori_loop(0, 3, tile, 0)
+        lax.fori_loop(0, 3, tile, 0, unroll=True)
         columns(pl.ds(1536, 128))
 
     def grads(kind, slot, slots=1):

time: 109 us -> 109 us (level)
  no operation moved by 1% of the time
where the time goes in v10:
time: 109 us; the launch traced here: 108 us
  Pallas kernels  105 us (96%)
  local copies, waits for them, and re-layouts  2.8 us (3%)
    pallas_call x1, Pallas kernels, body(): pl.pallas_call(kernel, out_shape=(jax.ShapeDtypeStruct((TOK, D), BF16), j...  105 us
    unnamed x5, local copies, waits for them, and re-layouts  2.8 us

profile of v10, /device:TPU:1, one launch (start us, length us, event | category | flops | bytes accessed | tf_op | source)
XLA Modules:
  0.0 108.2 jit_solution(9711399276607940769)
XLA Ops:
  0.6 0.0 copy-start
  0.6 0.7 copy-done
  1.3 104.8 %block_backward.1 = (bf16[128,1664]{1,0:T(8,128)(2,1)S(1)}, f32[400,104]{1,0:T(8,128)S(1)}, f32[400,104]{1,0:T(8,128)S(1)}) custom-call(bf16[128,1664]{1,0:T(8,128)(2,1)} %x_hbm.1, bf16[128,1664]{1,0:T(8,128)(2,1)} %up_hbm.1, bf16[1664]{0:T(1024)(128)(2,1)S(1)} %copy-done, bf16[400,1664]{1,0:T(8,128)(2,1)} %bitcast.3, bf16[400,1664]{1,0:T(8,128)(2,1)} %wd_hbm.1), custom_call_target="tpu_custom_call" | custom-call | tf_op jit(solution)/shard_map/block_backward/pallas_call | solution.py:561
  106.1 0.8 copy.11
  106.9 0.7 copy.12
  107.6 0.7 copy.13
Async XLA Ops:
  0.6 0.7 copy-start
